TPU v7x, 512 devices: a whole 4x4x16 slice. The times are simulated.
512 devices in a mesh: row: 4 (over y_lo, core), col: 16 (over z), depth: 8 (over x, y_hi).
Axes of the slice: x: 4, y: 4 (y_hi: 2, y_lo: 2; y = y_hi * 2 + y_lo), z: 16, core: 2. Of those that a mesh axis runs over, the one named last changes fastest.
Arguments:
- lower_block: bfloat16 [24576, 2048], P(('col', 'row')), may hold values from -0.3984375 to 0.3984375
- solve_factor: bfloat16 [2048, 2048], P(None, 'depth'), may hold values from -0.125 to 0.125
- schur_window: float32 [2560, 24576], P(('row', 'depth'), 'col'), may hold values from -6 to 6
Outputs:
- schur: float32 [2560, 24576], P(('row', 'depth'), 'col')
All inputs are finite; a program needn't handle non-finite values.
Results may differ from a plain program's by a relative error of at most 0.0003.
Values may be sent and summed in bfloat16 or wider, within the bound.
No kernel may reach another device: no remote copies, remote signals or barrier semaphores. Data moves between devices by JAX's collectives and lax.ppermute only.
A program may use at most 64 MiB of HBM per device.

v0:
```python
import jax
import jax.numpy as jnp
from jax import lax
from jax.sharding import PartitionSpec as P


def transposed_product(left, right):
    return lax.dot_general(
        left, right, (((1,), (1,)), ((), ())), preferred_element_type=jnp.float32
    )


def on_device(lower_block, solve_factor, schur_window):
    panel = jnp.dot(lower_block, solve_factor, preferred_element_type=jnp.float32).astype(
        jnp.bfloat16
    )
    win_rows = schur_window.shape[0]
    window_rows = lax.all_gather(
        panel[: win_rows * lax.axis_size("depth") // lax.axis_size("col")],
        "col",
        axis=0,
        tiled=True,
    )
    terms = transposed_product(window_rows, lax.all_gather(panel, "row", axis=0, tiled=True))
    update = lax.psum_scatter(terms, "depth", scatter_dimension=0, tiled=True)
    return schur_window - update


def solution(mesh):
    placed = (P(("col", "row"), None), P(None, "depth"), P(("row", "depth"), "col"))
    return jax.shard_map(
        on_device, mesh=mesh, in_specs=placed, out_specs=P(("row", "depth"), "col"), check_vma=False
    )
```

profile of v0, /device:TPU:6, one launch (start us, length us, event | category | flops | bytes accessed | tf_op | source)
XLA Modules:
  0.0 162.1 jit_solution(14656735473810589671)
XLA Ops:
  6.5 0.0 copy-start
  6.5 0.0 reduce-scatter.2.cloned.1.call-start
  6.5 1.4 copy-done
  7.9 1.8 %convolution_convert_fusion = bf16[384,256]{1,0:T(8,128)(2,1)S(1)} fusion(bf16[384,2048]{1,0:T(8,128)(2,1)S(1)} %copy-done, bf16[2048,256]{1,0:T(8,128)(2,1)} %param.4), kind=kOutput, calls=%fused_computation | convolution fusion | flops 402751488 | bytes 2818048 | tf_op jit(solution)/shard_map/dot_general | solution.py:14
  9.8 8.7 %all_gather.7 = bf16[1536,256]{1,0:T(8,128)(2,1)S(1)} all-gather(bf16[384,256]{1,0:T(8,128)(2,1)S(1)} %convolution_convert_fusion), channel_id=1, replica_groups=mesh['row'=4,'col'=16,'depth'=8] {'row'}, dimensions={0}, use_global_device_ids=true | all-gather | bytes 983040 | tf_op jit(solution)/shard_map/all_gather | solution.py:24
  18.4 37.1 %all_gather.6 = bf16[640,256]{1,0:T(8,128)(2,1)S(1)} all-gather(bf16[40,256]{1,0:T(8,128)(2,1)S(1)} %slice.4), channel_id=1, replica_groups=mesh['row'=4,'col'=16,'depth'=8] {'col'}, dimensions={0}, use_global_device_ids=true | all-gather | bytes 348160 | tf_op jit(solution)/shard_map/all_gather | solution.py:18
  55.6 2.6 %fusion = f32[640,1536]{1,0:T(8,128)} fusion(bf16[640,256]{1,0:T(8,128)(2,1)S(1)} %all_gather.6, bf16[1536,256]{1,0:T(8,128)(2,1)S(1)} %all_gather.7), kind=kOutput, calls=%fused_computation.1 | convolution fusion | flops 503316480 | bytes 5046272 | tf_op jit(solution)/shard_map/dot_general | solution.py:8
  58.1 0.0 copy-start.1
  58.1 0.0 reduce-scatter.2.cloned.1.call-update
  58.2 95.2 %reduce-scatter.2.cloned.1.call-done = f32[80,1536]{1,0:T(8,128)} async-done(((f32[640,1536]{1,0:T(8,128)}), f32[80,1536]{1,0:T(8,128)}) %reduce-scatter.2.cloned.1.call-update) | async-done | bytes 491536 | tf_op jit(solution)/shard_map/reduce_scatter | solution.py:25
  153.4 0.0 copy-done.1
  153.4 1.9 %sub.3 = f32[80,1536]{1,0:T(8,128)} subtract(f32[80,1536]{1,0:T(8,128)S(1)} %copy-done.1, f32[80,1536]{1,0:T(8,128)} %reduce-scatter.2.cloned.1.call-done) | non-fusion elementwise | flops 122880 | bytes 1474560 | tf_op jit(solution)/shard_map/sub | solution.py:26
  (1 shorter events, 0.0 us)
Async XLA Ops:
  6.5 1.4 copy-start
  6.5 146.8 %reduce-scatter.2.cloned.1.call-start = ((), (), s32[]{:S(2)}) async-start(), calls=%async_computation.1 | async-start | bytes 4423680 | tf_op jit(solution)/shard_map/reduce_scatter | solution.py:25
  58.1 95.2 %copy-start.1 = (f32[80,1536]{1,0:T(8,128)S(1)}, f32[80,1536]{1,0:T(8,128)}, u32[]{:S(2)}) copy-start(f32[80,1536]{1,0:T(8,128)} %param.5) | copy-start | bytes 1474564
Sparse Core Ops, SparseCore 0:
  58.3 95.0 reduce-scatter.1
where the time goes:
time: 162 us
  waiting for transfers between devices  95.2 us (59%)
  blocking collectives  45.8 us (28%)
  between operations  13.4 us (8%)
  matrix products  4.37 us (3%)
  other arithmetic  1.86 us (1%)
    reduce_scatter x1, waiting for transfers between devices, on_device(): update = lax.psum_scatter(terms, 'depth', scatter_dimension=0, tiled=True)  95.2 us
    all_gather x1, blocking collectives, on_device(): lax.all_gather(panel[:win_rows * lax.axis_size('depth') // lax.axis_size(...  37.1 us
    all_gather x1, blocking collectives, on_device(): lax.all_gather(panel, 'row', axis=0, tiled=True)  8.68 us
  transfers between devices with their start and end apart: 1, of which 1 were waited for; matrix products, arithmetic and copies ran while one was open for 0% of the time, Pallas kernels for 0%

commit v1 on v0

v1 whole, which is shorter than its diff:
```python
import jax
import jax.numpy as jnp
from jax import lax
from jax.sharding import Mesh, PartitionSpec as P

AXES = ("ylo", "core", "zh", "zl", "x", "yhi")


def spread(block, axes, parts):
    copies = jnp.broadcast_to(block[None], (parts,) + block.shape)
    return lax.all_to_all(copies, axes, 0, 0, tiled=True)


SWAP = ((0, 1), (1, 0))


def shifts(size):
    return [[(i, (i + k) % size) for i in range(size)] for k in range(1, size)]


def on_device(lower_block, solve_factor, schur_window):
    panel = jnp.dot(lower_block, solve_factor, preferred_element_type=jnp.float32).astype(jnp.bfloat16)
    win = 40
    near = spread(panel, ("ylo", "x", "yhi"), 16)
    w = lax.all_gather(panel[:win], "zh")
    w = lax.all_gather(w, "zl")
    w = w.reshape(2, 2, 4, win, 256).transpose(0, 2, 1, 3, 4).reshape(2, 4, 2 * win, 256)
    h = lax.axis_index("yhi")
    got = lax.ppermute(lax.dynamic_index_in_dim(w, 1 - h, 0, False), "yhi", SWAP)
    own = lax.dynamic_index_in_dim(w, h, 0, False)
    lo, hi = jnp.where(h == 0, own, got), jnp.where(h == 0, got, own)
    w = jnp.stack([lo, hi], 1)
    x = lax.axis_index("x")
    parts = [lax.dynamic_index_in_dim(w, x, 0, False)]
    for k, perm in enumerate(shifts(4), 1):
        parts.append(lax.ppermute(lax.dynamic_index_in_dim(w, (x + k) % 4, 0, False), "x", perm))
    w = jnp.stack(parts)
    w = jnp.roll(w[::-1], x + 1, 0).reshape(8, 2 * win, 256)
    other_w = lax.ppermute(w, "core", SWAP)
    near = near.reshape(2, 8, 384, 256)
    rows = jnp.concatenate([w, other_w], 1)
    prod = lax.dot_general(rows, near, (((0, 2), (1, 3)), ((), ())), preferred_element_type=jnp.float32)
    mine = prod[:80]
    theirs = lax.ppermute(prod[80:], "core", SWAP)
    first = lax.axis_index("core") == 0
    update = jnp.stack([jnp.where(first, mine, theirs), jnp.where(first, theirs, mine)], 2)
    return schur_window - update.reshape(schur_window.shape)


def solution(mesh):
    fine = Mesh(mesh.devices.reshape(2, 2, 4, 4, 4, 2), AXES)
    z, row, depth = ("zh", "zl"), ("ylo", "core"), ("x", "yhi")
    out = P(row + depth, z)
    return jax.shard_map(
        on_device, mesh=fine, in_specs=(P(z + row, None), P(None, depth), out), out_specs=out, check_vma=False
    )
```

time: 162 us -> 92.9 us (0.57)
  the two profiles are of different devices: /device:TPU:6 before, /device:TPU:449 now
where the time goes in v1:
time: 92.9 us; the launch traced here: 92.4 us
  starting transfers between devices  29.8 us (32%)
  waiting for transfers between devices  26.1 us (28%)
  blocking collectives  25.9 us (28%)
  matrix products  4.84 us (5%)
  local copies, waits for them, and re-layouts  4.44 us (5%)
  other arithmetic  1.15 us (1%)
    ppermute x1, waiting for transfers between devices, on_device(): lax.ppermute(lax.dynamic_index_in_dim(w, 1 - h, 0, False), 'yhi', SWAP)  18.6 us
    all_gather x1, blocking collectives, on_device(): w = lax.all_gather(panel[:win], 'zh')  14.5 us
    all_gather x1, blocking collectives, on_device(): w = lax.all_gather(w, 'zl')  11.4 us
    ppermute x3, starting transfers between devices, on_device(): lax.ppermute(lax.dynamic_index_in_dim(w, (x + k) % 4, 0, False), 'x', perm)  11.4 us
    all_to_all x1, starting transfers between devices, spread(): return lax.all_to_all(copies, axes, 0, 0, tiled=True)  6.8 us
    ppermute x3, waiting for transfers between devices, on_device(): lax.ppermute(lax.dynamic_index_in_dim(w, (x + k) % 4, 0, False), 'x', perm)  5.08 us
    ppermute x1, starting transfers between devices, on_device(): lax.ppermute(lax.dynamic_index_in_dim(w, 1 - h, 0, False), 'yhi', SWAP)  4.84 us
    ppermute x1, starting transfers between devices, on_device(): other_w = lax.ppermute(w, 'core', SWAP)  4.49 us
  transfers between devices with their start and end apart: 7, of which 5 were waited for; matrix products, arithmetic and copies ran while one was open for 0% of the time, Pallas kernels for 0%

profile of v1, /device:TPU:449, one launch (start us, length us, event | category | flops | bytes accessed | tf_op | source)
XLA Modules:
  0.0 92.4 jit_solution(17217585628535095781)
XLA Ops:
  0.0 0.0 copy-start
  0.0 1.4 %copy-done = bf16[384,2048]{1,0:T(8,128)(2,1)S(1)} copy-done((bf16[384,2048]{1,0:T(8,128)(2,1)S(1)}, bf16[384,2048]{1,0:T(8,128)(2,1)}, u32[]{:S(2)}) %copy-start) | copy-done | bytes 1572888
  1.4 1.8 %convolution_convert_fusion = bf16[384,256]{1,0:T(8,128)(2,1)S(1)} fusion(bf16[384,2048]{1,0:T(8,128)(2,1)S(1)} %copy-done, bf16[2048,256]{1,0:T(8,128)(2,1)} %param.4), kind=kOutput, calls=%fused_computation.1 | convolution fusion | flops 402751488 | bytes 2818048 | tf_op jit(solution)/shard_map/dot_general | solution.py:22
  3.2 2.0 %broadcast_in_dim.2 = bf16[16,384,256]{2,1,0:T(8,128)(2,1)} broadcast(bf16[384,256]{1,0:T(8,128)(2,1)S(1)} %convolution_convert_fusion), dimensions={1,2} | broadcast | bytes 3342336 | tf_op jit(solution)/shard_map/broadcast_in_dim | solution.py:10
  5.2 6.8 %all-to-all-start = ((bf16[16,384,256]{2,1,0:T(8,128)(2,1)}), bf16[16,384,256]{2,1,0:T(8,128)(2,1)}, u32[]{:S(2)}, u32[]{:S(2)}) async-start(bf16[16,384,256]{2,1,0:T(8,128)(2,1)} %broadcast_in_dim.2), calls=%async_computation | async-start | bytes 6291456 | tf_op jit(solution)/shard_map/all_to_all | solution.py:11
  12.0 14.5 %all-gather = bf16[160,256]{1,0:T(8,128)(2,1)S(1)} all-gather(bf16[40,256]{1,0:T(8,128)(2,1)S(1)} %slice.12), channel_id=2, replica_groups=mesh['ylo'=2,'core'=2,'zh'=4,'zl'=4,'x'=4,'yhi'=2] {'zh'}, dimensions={0}, use_global_device_ids=true | all-gather | bytes 102400 | tf_op jit(solution)/shard_map/all_gather | solution.py:25
  26.5 11.4 %all-gather.1 = bf16[16,40,256]{2,1,0:T(8,128)(2,1)S(1)} all-gather(bf16[4,40,256]{2,1,0:T(8,128)(2,1)S(1)} %bitcast.49), channel_id=3, replica_groups=mesh['ylo'=2,'core'=2,'zh'=4,'zl'=4,'x'=4,'yhi'=2] {'zl'}, dimensions={0}, use_global_device_ids=true | all-gather | bytes 409600 | tf_op jit(solution)/shard_map/all_gather | solution.py:26
  38.0 4.8 %collective-permute-start = (bf16[4,80,256]{2,1,0:T(8,128)(2,1)S(1)}, bf16[4,80,256]{2,1,0:T(8,128)(2,1)S(1)}, u32[]{:S(2)}, u32[]{:S(2)}) collective-permute-start(bf16[4,80,256]{2,1,0:T(8,128)(2,1)S(1)} %dynamic-slice_bitcast_fusion), channel_id=1, source_target_pairs={{0,1},{1,0},{2,3},{3,2},{4,5},{5,4},{6,7},{7,6},{8,9},{9,8},{10,11... | collective-permute-start | bytes 491528 | tf_op jit(solution)/shard_map/ppermute | solution.py:29
  42.9 18.6 %collective-permute-done = bf16[4,80,256]{2,1,0:T(8,128)(2,1)S(1)} collective-permute-done((bf16[4,80,256]{2,1,0:T(8,128)(2,1)S(1)}, bf16[4,80,256]{2,1,0:T(8,128)(2,1)S(1)}, u32[]{:S(2)}, u32[]{:S(2)}) %collective-permute-start) | collective-permute-done | bytes 163872 | tf_op jit(solution)/shard_map/ppermute | solution.py:29
  61.6 6.1 %collective-permute-start.3 = (bf16[2,80,256]{2,1,0:T(8,128)(2,1)S(1)}, bf16[2,80,256]{2,1,0:T(8,128)(2,1)S(1)}, u32[]{:S(2)}, u32[]{:S(2)}) collective-permute-start(bf16[2,80,256]{2,1,0:T(8,128)(2,1)S(1)} %get-tuple-element.12), channel_id=1, source_target_pairs={{0,6},{2,0},{4,2},{6,4},{1,7},{3,1},{5,3},{7,5},{8,14},{10,8},{12,... | collective-permute-start | bytes 245768 | tf_op jit(solution)/shard_map/ppermute | solution.py:36
  67.7 3.4 %collective-permute-start.2 = (bf16[2,80,256]{2,1,0:T(8,128)(2,1)S(1)}, bf16[2,80,256]{2,1,0:T(8,128)(2,1)S(1)}, u32[]{:S(2)}, u32[]{:S(2)}) collective-permute-start(bf16[2,80,256]{2,1,0:T(8,128)(2,1)S(1)} %get-tuple-element.11), channel_id=1, source_target_pairs={{0,4},{2,6},{4,0},{6,2},{1,5},{3,7},{5,1},{7,3},{8,12},{10,14},{12... | collective-permute-start | bytes 245768 | tf_op jit(solution)/shard_map/ppermute | solution.py:36
  71.1 1.9 %collective-permute-start.1 = (bf16[2,80,256]{2,1,0:T(8,128)(2,1)S(1)}, bf16[2,80,256]{2,1,0:T(8,128)(2,1)S(1)}, u32[]{:S(2)}, u32[]{:S(2)}) collective-permute-start(bf16[2,80,256]{2,1,0:T(8,128)(2,1)S(1)} %get-tuple-element.10), channel_id=1, source_target_pairs={{0,2},{2,4},{4,6},{6,0},{1,3},{3,5},{5,7},{7,1},{8,10},{10,12},{12... | collective-permute-start | bytes 245768 | tf_op jit(solution)/shard_map/ppermute | solution.py:36
  73.0 0.0 collective-permute-done.3
  73.0 1.4 %collective-permute-done.2 = bf16[2,80,256]{2,1,0:T(8,128)(2,1)S(1)} collective-permute-done((bf16[2,80,256]{2,1,0:T(8,128)(2,1)S(1)}, bf16[2,80,256]{2,1,0:T(8,128)(2,1)S(1)}, u32[]{:S(2)}, u32[]{:S(2)}) %collective-permute-start.2) | collective-permute-done | bytes 81952 | tf_op jit(solution)/shard_map/ppermute | solution.py:36
  74.4 3.7 %collective-permute-done.1 = bf16[2,80,256]{2,1,0:T(8,128)(2,1)S(1)} collective-permute-done((bf16[2,80,256]{2,1,0:T(8,128)(2,1)S(1)}, bf16[2,80,256]{2,1,0:T(8,128)(2,1)S(1)}, u32[]{:S(2)}, u32[]{:S(2)}) %collective-permute-start.1) | collective-permute-done | bytes 81952 | tf_op jit(solution)/shard_map/ppermute | solution.py:36
  78.2 0.1 fusion.2
  78.3 4.5 %collective-permute-start.4 = (bf16[8,80,256]{2,1,0:T(8,128)(2,1)S(1)}, bf16[8,80,256]{2,1,0:T(8,128)(2,1)S(1)}, u32[]{:S(2)}, u32[]{:S(2)}) collective-permute-start(bf16[8,80,256]{2,1,0:T(8,128)(2,1)S(1)} %bitcast.47), channel_id=1, source_target_pairs={{0,128},{128,0},{1,129},{129,1},{2,130},{130,2},{3,131},{131,3},{4... | collective-permute-start | bytes 983048 | tf_op jit(solution)/shard_map/ppermute | solution.py:39
  82.8 1.2 %collective-permute-done.4 = bf16[8,80,256]{2,1,0:T(8,128)(2,1)S(1)} collective-permute-done((bf16[8,80,256]{2,1,0:T(8,128)(2,1)S(1)}, bf16[8,80,256]{2,1,0:T(8,128)(2,1)S(1)}, u32[]{:S(2)}, u32[]{:S(2)}) %collective-permute-start.4) | collective-permute-done | bytes 327712 | tf_op jit(solution)/shard_map/ppermute | solution.py:39
  84.1 0.0 all-to-all-done
  84.1 3.0 %convolution_bitcast_fusion = f32[160,2,384]{2,0,1:T(8,128)S(1)} fusion(bf16[2,8,384,256]{3,2,1,0:T(8,128)(2,1)} %bitcast.17, bf16[8,80,256]{2,1,0:T(8,128)(2,1)S(1)} %collective-permute-done.4, bf16[8,80,256]{2,1,0:T(8,128)(2,1)S(1)} %bitcast.48), kind=kOutput, calls=%fused_computation | convolution fusion | flops 504627200 | bytes 4292608 | tf_op jit(solution)/shard_map/dot_general | solution.py:42
  87.1 2.3 %collective-permute-start.5 = (f32[80,2,384]{2,0,1:T(8,128)S(1)}, f32[80,2,384]{2,0,1:T(8,128)S(1)}, u32[]{:S(2)}, u32[]{:S(2)}) collective-permute-start(f32[80,2,384]{2,0,1:T(8,128)S(1)} %slice.14), channel_id=1, source_target_pairs={{0,128},{128,0},{1,129},{129,1},{2,130},{130,2},{3,131},{131,3},{4... | collective-permute-start | bytes 737288 | tf_op jit(solution)/shard_map/ppermute | solution.py:44
  89.4 1.1 %collective-permute-done.5 = f32[80,2,384]{2,0,1:T(8,128)S(1)} collective-permute-done((f32[80,2,384]{2,0,1:T(8,128)S(1)}, f32[80,2,384]{2,0,1:T(8,128)S(1)}, u32[]{:S(2)}, u32[]{:S(2)}) %collective-permute-start.5) | collective-permute-done | bytes 245792 | tf_op jit(solution)/shard_map/ppermute | solution.py:44
  90.6 0.0 copy-start.1
  90.6 0.4 copy.12
  91.0 0.4 reshape.20
  91.4 0.2 copy-done.1
  91.6 0.8 sub.12
  (10 shorter events, 0.3 us)
Async XLA Ops:
  0.0 1.4 %copy-start = (bf16[384,2048]{1,0:T(8,128)(2,1)S(1)}, bf16[384,2048]{1,0:T(8,128)(2,1)}, u32[]{:S(2)}) copy-start(bf16[384,2048]{1,0:T(8,128)(2,1)} %param.3) | copy-start | bytes 4718596
  5.2 78.9 %all-to-all-start = ((bf16[16,384,256]{2,1,0:T(8,128)(2,1)}), bf16[16,384,256]{2,1,0:T(8,128)(2,1)}, u32[]{:S(2)}, u32[]{:S(2)}) async-start(bf16[16,384,256]{2,1,0:T(8,128)(2,1)} %broadcast_in_dim.2), calls=%async_computation | async-start | bytes 6291456 | tf_op jit(solution)/shard_map/all_to_all | solution.py:11
  38.0 23.5 %collective-permute-start = (bf16[4,80,256]{2,1,0:T(8,128)(2,1)S(1)}, bf16[4,80,256]{2,1,0:T(8,128)(2,1)S(1)}, u32[]{:S(2)}, u32[]{:S(2)}) collective-permute-start(bf16[4,80,256]{2,1,0:T(8,128)(2,1)S(1)} %dynamic-slice_bitcast_fusion), channel_id=1, source_target_pairs={{0,1},{1,0},{2,3},{3,2},{4,5},{5,4},{6,7},{7,6},{8,9},{9,8},{10,11... | collective-permute-start | bytes 491528 | tf_op jit(solution)/shard_map/ppermute | solution.py:29
  61.6 11.4 %collective-permute-start.3 = (bf16[2,80,256]{2,1,0:T(8,128)(2,1)S(1)}, bf16[2,80,256]{2,1,0:T(8,128)(2,1)S(1)}, u32[]{:S(2)}, u32[]{:S(2)}) collective-permute-start(bf16[2,80,256]{2,1,0:T(8,128)(2,1)S(1)} %get-tuple-element.12), channel_id=1, source_target_pairs={{0,6},{2,0},{4,2},{6,4},{1,7},{3,1},{5,3},{7,5},{8,14},{10,8},{12,... | collective-permute-start | bytes 245768 | tf_op jit(solution)/shard_map/ppermute | solution.py:36
  67.7 6.7 %collective-permute-start.2 = (bf16[2,80,256]{2,1,0:T(8,128)(2,1)S(1)}, bf16[2,80,256]{2,1,0:T(8,128)(2,1)S(1)}, u32[]{:S(2)}, u32[]{:S(2)}) collective-permute-start(bf16[2,80,256]{2,1,0:T(8,128)(2,1)S(1)} %get-tuple-element.11), channel_id=1, source_target_pairs={{0,4},{2,6},{4,0},{6,2},{1,5},{3,7},{5,1},{7,3},{8,12},{10,14},{12... | collective-permute-start | bytes 245768 | tf_op jit(solution)/shard_map/ppermute | solution.py:36
  71.1 7.0 %collective-permute-start.1 = (bf16[2,80,256]{2,1,0:T(8,128)(2,1)S(1)}, bf16[2,80,256]{2,1,0:T(8,128)(2,1)S(1)}, u32[]{:S(2)}, u32[]{:S(2)}) collective-permute-start(bf16[2,80,256]{2,1,0:T(8,128)(2,1)S(1)} %get-tuple-element.10), channel_id=1, source_target_pairs={{0,2},{2,4},{4,6},{6,0},{1,3},{3,5},{5,7},{7,1},{8,10},{10,12},{12... | collective-permute-start | bytes 245768 | tf_op jit(solution)/shard_map/ppermute | solution.py:36
  78.3 5.7 %collective-permute-start.4 = (bf16[8,80,256]{2,1,0:T(8,128)(2,1)S(1)}, bf16[8,80,256]{2,1,0:T(8,128)(2,1)S(1)}, u32[]{:S(2)}, u32[]{:S(2)}) collective-permute-start(bf16[8,80,256]{2,1,0:T(8,128)(2,1)S(1)} %bitcast.47), channel_id=1, source_target_pairs={{0,128},{128,0},{1,129},{129,1},{2,130},{130,2},{3,131},{131,3},{4... | collective-permute-start | bytes 983048 | tf_op jit(solution)/shard_map/ppermute | solution.py:39
  87.1 3.4 %collective-permute-start.5 = (f32[80,2,384]{2,0,1:T(8,128)S(1)}, f32[80,2,384]{2,0,1:T(8,128)S(1)}, u32[]{:S(2)}, u32[]{:S(2)}) collective-permute-start(f32[80,2,384]{2,0,1:T(8,128)S(1)} %slice.14), channel_id=1, source_target_pairs={{0,128},{128,0},{1,129},{129,1},{2,130},{130,2},{3,131},{131,3},{4... | collective-permute-start | bytes 737288 | tf_op jit(solution)/shard_map/ppermute | solution.py:44
  90.6 1.0 %copy-start.1 = (f32[80,1536]{1,0:T(8,128)S(1)}, f32[80,1536]{1,0:T(8,128)}, u32[]{:S(2)}) copy-start(f32[80,1536]{1,0:T(8,128)} %param.5) | copy-start | bytes 1474564

commit v2 on v1

v2 whole, which is shorter than its diff:
```python
import jax
import jax.numpy as jnp
from jax import lax
from jax.experimental import pallas as pl
from jax.experimental.pallas import tpu as pltpu
from jax.sharding import Mesh, PartitionSpec as P

AXES = ("ylo", "core", "zh", "zl", "x", "yhi")
WIN = 40
SWAP = ((0, 1), (1, 0))


def product_kernel(at_ref, w, mine, theirs, out_ref, rows_ref):
    h, b = at_ref[0], at_ref[1]
    for p in range(4):
        start = pl.multiple_of(((p // 2 + h) % 2) * 2 * WIN + (p % 2) * WIN, 8)
        for x in range(4):
            rows_ref[x, pl.ds(start, WIN), :] = w[p, x].astype(jnp.float32)
    for a in range(2):
        for t, near in enumerate((mine, theirs)):
            total = None
            for x in range(4):
                term = lax.dot_general(
                    rows_ref[x].astype(jnp.bfloat16), near[a, x], (((1,), (1,)), ((), ())), preferred_element_type=jnp.float32
                )
                total = term if total is None else total + term
            cols = pl.multiple_of(a * 768 + ((b + t) % 2) * 384, 128)
            out_ref[0, :, pl.ds(cols, 384)] = total[:80]
            out_ref[1, :, pl.ds(cols, 384)] = total[80:]


def product(at, w, mine, theirs):
    return pl.pallas_call(
        product_kernel,
        out_shape=jax.ShapeDtypeStruct((2, 2 * WIN, 1536), jnp.float32),
        in_specs=[pl.BlockSpec(memory_space=pltpu.SMEM)] + [pl.BlockSpec(memory_space=pltpu.VMEM)] * 3,
        out_specs=pl.BlockSpec(memory_space=pltpu.VMEM),
        scratch_shapes=[pltpu.VMEM((4, 4 * WIN, 256), jnp.float32)],
        compiler_params=pltpu.CompilerParams(vmem_limit_bytes=32 * 2**20),
        cost_estimate=pl.CostEstimate(flops=2 * 160 * 1536 * 1024, bytes_accessed=4 * 2**20, transcendentals=0),
    )(at, w, mine, theirs)


def spread(block, axes, parts):
    copies = jnp.broadcast_to(block[None], (parts,) + block.shape)
    return lax.all_to_all(copies, axes, 0, 0, tiled=True)


def dot(left, right):
    return jnp.dot(left, right, preferred_element_type=jnp.float32).astype(jnp.bfloat16)


def shift(size, k):
    return [(i, (i + k) % size) for i in range(size)]


def on_device(lower_block, solve_factor, schur_window):
    h, b = lax.axis_index("yhi"), lax.axis_index("core")
    panel = dot(lower_block, solve_factor)
    near = spread(panel, ("ylo", "x"), 8).reshape(2, 4, 384, 256)
    w = lax.all_gather(panel[:WIN], ("zh", "zl"))
    near, w = lax.optimization_barrier((near, w))
    w = w.reshape(4, 4, WIN, 256).transpose(1, 0, 2, 3)
    w = lax.all_to_all(w, "x", 1, 1, tiled=True)
    other = lax.ppermute(near, "core", SWAP)
    out = product(jnp.stack([h, b]), w, near, other)
    return schur_window - (out[0] + lax.ppermute(out[1], "yhi", SWAP))


def solution(mesh):
    fine = Mesh(mesh.devices.reshape(2, 2, 4, 4, 4, 2), AXES)
    z, row, depth = ("zh", "zl"), ("ylo", "core"), ("x", "yhi")
    out = P(row + depth, z)
    return jax.shard_map(
        on_device, mesh=fine, in_specs=(P(z + row, None), P(None, depth), out), out_specs=out, check_vma=False
    )
```

time: 92.9 us -> 83.8 us (0.902)
  the two profiles are of different devices: /device:TPU:449 before, /device:TPU:24 now
where the time goes in v2:
time: 83.8 us; the launch traced here: 83.5 us
  blocking collectives  39.8 us (47%)
  waiting for transfers between devices  20.7 us (25%)
  starting transfers between devices  14.8 us (18%)
  local copies, waits for them, and re-layouts  2.72 us (3%)
  Pallas kernels  2.58 us (3%)
  matrix products  1.79 us (2%)
  other arithmetic  0.93 us (1%)
    all_gather x1, blocking collectives, on_device(): w = lax.all_gather(panel[:WIN], ('zh', 'zl'))  39.8 us
    ppermute x1, waiting for transfers between devices, on_device(): return schur_window - (out[0] + lax.ppermute(out[1], 'yhi', SWAP))  12.8 us
    all_to_all x1, waiting for transfers between devices, on_device(): w = lax.all_to_all(w, 'x', 1, 1, tiled=True)  7.96 us
    all_to_all x1, starting transfers between devices, spread(): return lax.all_to_all(copies, axes, 0, 0, tiled=True)  5.76 us
    all_to_all x1, starting transfers between devices, on_device(): w = lax.all_to_all(w, 'x', 1, 1, tiled=True)  3.98 us
    ppermute x1, starting transfers between devices, on_device(): return schur_window - (out[0] + lax.ppermute(out[1], 'yhi', SWAP))  3.14 us
    pallas_call x1, Pallas kernels, product(): pl.pallas_call(product_kernel, out_shape=jax.ShapeDtypeStruct((2, 2 * WIN...  2.58 us
    ppermute x1, starting transfers between devices, on_device(): other = lax.ppermute(near, 'core', SWAP)  1.91 us
  transfers between devices with their start and end apart: 4, of which 2 were waited for; matrix products, arithmetic and copies ran while one was open for 0% of the time, Pallas kernels for 0%

profile of v2, /device:TPU:24, one launch (start us, length us, event | category | flops | bytes accessed | tf_op | source)
XLA Modules:
  0.0 83.5 jit_solution(11338511072287022871)
XLA Ops:
  0.0 0.0 copy-start
  0.0 1.4 %copy-done = bf16[384,2048]{1,0:T(8,128)(2,1)S(1)} copy-done((bf16[384,2048]{1,0:T(8,128)(2,1)S(1)}, bf16[384,2048]{1,0:T(8,128)(2,1)}, u32[]{:S(2)}) %copy-start) | copy-done | bytes 1572888
  1.4 1.8 %convolution_convert_fusion = bf16[384,256]{1,0:T(8,128)(2,1)S(1)} fusion(bf16[384,2048]{1,0:T(8,128)(2,1)S(1)} %copy-done, bf16[2048,256]{1,0:T(8,128)(2,1)} %param.4), kind=kOutput, calls=%fused_computation | convolution fusion | flops 402751488 | bytes 2818048 | tf_op jit(solution)/shard_map/dot_general | solution.py:50
  3.2 1.2 %broadcast_in_dim.2 = bf16[8,384,256]{2,1,0:T(8,128)(2,1)} broadcast(bf16[384,256]{1,0:T(8,128)(2,1)S(1)} %convolution_convert_fusion), dimensions={1,2} | broadcast | bytes 1769472 | tf_op jit(solution)/shard_map/broadcast_in_dim | solution.py:45
  4.5 5.8 %all-to-all-start = ((bf16[8,384,256]{2,1,0:T(8,128)(2,1)}), bf16[8,384,256]{2,1,0:T(8,128)(2,1)S(1)}, u32[]{:S(2)}, u32[]{:S(2)}) async-start(bf16[8,384,256]{2,1,0:T(8,128)(2,1)} %broadcast_in_dim.2), calls=%async_computation | async-start | bytes 3145728 | tf_op jit(solution)/shard_map/all_to_all | solution.py:46
  10.2 39.8 %all-gather = bf16[640,256]{1,0:T(8,128)(2,1)} all-gather(bf16[40,256]{1,0:T(8,128)(2,1)S(1)} %slice.12), channel_id=2, replica_groups=mesh['ylo'=2,'core'=2,'zh'=4,'zl'=4,'x'=4,'yhi'=2] {'zh','zl'}, dimensions={0}, use_global_device_ids=true | all-gather | bytes 348160 | tf_op jit(solution)/shard_map/all_gather | solution.py:61
  50.1 0.0 all-to-all-done
  50.1 1.9 %collective-permute-start = (bf16[2,4,384,256]{3,2,1,0:T(8,128)(2,1)S(1)}, bf16[2,4,384,256]{3,2,1,0:T(8,128)(2,1)}, u32[]{:S(2)}, u32[]{:S(2)}) collective-permute-start(bf16[2,4,384,256]{3,2,1,0:T(8,128)(2,1)S(1)} %bitcast.17), channel_id=1, source_target_pairs={{0,128},{128,0},{1,129},{129,1},{2,130},{130,2},{3,131},{131,3},{4... | collective-permute-start | bytes 4718600 | tf_op jit(solution)/shard_map/ppermute | solution.py:65
  52.0 4.0 %all-to-all-start.1 = ((bf16[4,4,40,256]{3,2,0,1:T(8,128)(2,1)}), bf16[4,4,40,256]{3,2,0,1:T(8,128)(2,1)S(1)}, u32[]{:S(2)}, u32[]{:S(2)}) async-start(bf16[4,4,40,256]{3,2,0,1:T(8,128)(2,1)} %bitcast.5), calls=%async_computation.1 | async-start | bytes 655360 | tf_op jit(solution)/shard_map/all_to_all | solution.py:64
  56.0 0.1 pad_add_fusion.at_ref
  56.0 8.0 %all-to-all-done.1 = bf16[4,4,40,256]{3,2,0,1:T(8,128)(2,1)S(1)} async-done(((bf16[4,4,40,256]{3,2,0,1:T(8,128)(2,1)}), bf16[4,4,40,256]{3,2,0,1:T(8,128)(2,1)S(1)}, u32[]{:S(2)}, u32[]{:S(2)}) %all-to-all-start.1) | async-done | bytes 327712 | tf_op jit(solution)/shard_map/all_to_all | solution.py:64
  64.0 0.0 copy-start.1
  64.0 0.0 collective-permute-done.theirs
  64.0 2.6 %shard_map.37 = f32[2,80,1536]{2,1,0:T(8,128)S(1)} custom-call(s32[2]{0:T(128)S(1)} %pad_add_fusion.at_ref, bf16[4,4,40,256]{3,2,1,0:T(8,128)(2,1)S(1)} %copy.5.w, bf16[2,4,384,256]{3,2,1,0:T(8,128)(2,1)S(1)} %bitcast.18, bf16[2,4,384,256]{3,2,1,0:T(8,128)(2,1)} %collective-permute-done.theirs), custom_call_target="tpu_custom_call" | custom-call | flops 503316480 | bytes 4194304 | tf_op jit(solution)/shard_map/pallas_call | solution.py:33
  66.7 3.1 %collective-permute-start.1 = (f32[80,1536]{1,0:T(8,128)S(1)}, f32[80,1536]{1,0:T(8,128)S(1)}, u32[]{:S(2)}, u32[]{:S(2)}) collective-permute-start(f32[80,1536]{1,0:T(8,128)S(1)} %slice_bitcast_fusion), channel_id=1, source_target_pairs={{0,1},{1,0},{2,3},{3,2},{4,5},{5,4},{6,7},{7,6},{8,9},{9,8},{10,11... | collective-permute-start | bytes 1474568 | tf_op jit(solution)/shard_map/ppermute | solution.py:67
  69.8 12.8 %collective-permute-done.1 = f32[80,1536]{1,0:T(8,128)S(1)} collective-permute-done((f32[80,1536]{1,0:T(8,128)S(1)}, f32[80,1536]{1,0:T(8,128)S(1)}, u32[]{:S(2)}, u32[]{:S(2)}) %collective-permute-start.1) | collective-permute-done | bytes 491552 | tf_op jit(solution)/shard_map/ppermute | solution.py:67
  82.6 0.0 copy-done.1
  82.6 0.9 %fusion.1 = f32[80,1536]{1,0:T(8,128)} fusion(f32[80,1536]{1,0:T(8,128)S(1)} %copy-done.1, f32[80,1536]{1,0:T(8,128)S(1)} %collective-permute-done.1, f32[2,80,1536]{2,1,0:T(8,128)S(1)} %shard_map.37), kind=kLoop, calls=%fused_computation.4 | loop fusion | flops 245760 | bytes 1966080 | tf_op jit(solution)/shard_map/sub | solution.py:67
  (3 shorter events, 0.1 us)
Async XLA Ops:
  0.0 1.4 %copy-start = (bf16[384,2048]{1,0:T(8,128)(2,1)S(1)}, bf16[384,2048]{1,0:T(8,128)(2,1)}, u32[]{:S(2)}) copy-start(bf16[384,2048]{1,0:T(8,128)(2,1)} %param.3) | copy-start | bytes 4718596
  4.5 45.6 %all-to-all-start = ((bf16[8,384,256]{2,1,0:T(8,128)(2,1)}), bf16[8,384,256]{2,1,0:T(8,128)(2,1)S(1)}, u32[]{:S(2)}, u32[]{:S(2)}) async-start(bf16[8,384,256]{2,1,0:T(8,128)(2,1)} %broadcast_in_dim.2), calls=%async_computation | async-start | bytes 3145728 | tf_op jit(solution)/shard_map/all_to_all | solution.py:46
  50.1 14.0 %collective-permute-start = (bf16[2,4,384,256]{3,2,1,0:T(8,128)(2,1)S(1)}, bf16[2,4,384,256]{3,2,1,0:T(8,128)(2,1)}, u32[]{:S(2)}, u32[]{:S(2)}) collective-permute-start(bf16[2,4,384,256]{3,2,1,0:T(8,128)(2,1)S(1)} %bitcast.17), channel_id=1, source_target_pairs={{0,128},{128,0},{1,129},{129,1},{2,130},{130,2},{3,131},{131,3},{4... | collective-permute-start | bytes 4718600 | tf_op jit(solution)/shard_map/ppermute | solution.py:65
  52.0 12.0 %all-to-all-start.1 = ((bf16[4,4,40,256]{3,2,0,1:T(8,128)(2,1)}), bf16[4,4,40,256]{3,2,0,1:T(8,128)(2,1)S(1)}, u32[]{:S(2)}, u32[]{:S(2)}) async-start(bf16[4,4,40,256]{3,2,0,1:T(8,128)(2,1)} %bitcast.5), calls=%async_computation.1 | async-start | bytes 655360 | tf_op jit(solution)/shard_map/all_to_all | solution.py:64
  64.0 18.6 %copy-start.1 = (f32[80,1536]{1,0:T(8,128)S(1)}, f32[80,1536]{1,0:T(8,128)}, u32[]{:S(2)}) copy-start(f32[80,1536]{1,0:T(8,128)} %param.5) | copy-start | bytes 1474564
  66.7 15.9 %collective-permute-start.1 = (f32[80,1536]{1,0:T(8,128)S(1)}, f32[80,1536]{1,0:T(8,128)S(1)}, u32[]{:S(2)}, u32[]{:S(2)}) collective-permute-start(f32[80,1536]{1,0:T(8,128)S(1)} %slice_bitcast_fusion), channel_id=1, source_target_pairs={{0,1},{1,0},{2,3},{3,2},{4,5},{5,4},{6,7},{7,6},{8,9},{9,8},{10,11... | collective-permute-start | bytes 1474568 | tf_op jit(solution)/shard_map/ppermute | solution.py:67

commit v3 on v0

v3 whole, which is shorter than its diff:
```python
import jax
import jax.numpy as jnp
from jax import lax
from jax.experimental import pallas as pl
from jax.experimental.pallas import tpu as pltpu
from jax.sharding import Mesh, PartitionSpec as P

AXES = ("ylo", "core", "z", "x", "yhi")
FIRST = 10
WIN = 40
SWAP = ((0, 1), (1, 0))
VMEM = pl.BlockSpec(memory_space=pltpu.VMEM)
SMEM = pl.BlockSpec(memory_space=pltpu.SMEM)


def product_kernel(at_ref, w, n00, n01, n10, n11, theirs, *refs):
    outs, rows_ref = refs[:4], refs[4]
    h, a, b, x = at_ref[0], at_ref[1], at_ref[2], at_ref[3]
    for dh in range(2):
        for k in range(4):
            for q in range(2):
                start = (k * 2 + q) * WIN
                rows_ref[dh, start : start + WIN, :] = w[q * 2 + (h + dh) % 2, (x + k) % 4].astype(jnp.float32)
    left = [rows_ref[dh].astype(jnp.bfloat16) for dh in range(2)]
    for da in range(2):
        for t in range(2):
            total = None
            for dh in range(2):
                near = theirs[dh * 2 + da] if t else ((n00, n01), (n10, n11))[dh][da][...]
                term = lax.dot_general(left[dh], near, (((1,), (1,)), ((), ())), preferred_element_type=jnp.float32)
                total = term if total is None else total + term
            cols = pl.multiple_of(((a + da) % 2) * 768 + ((b + t) % 2) * 384, 128)
            for k in range(4):
                outs[k][:, pl.ds(cols, 384)] = total[k * 2 * WIN : (k + 1) * 2 * WIN]


def product(at, w, near, theirs):
    part = jax.ShapeDtypeStruct((2 * WIN, 1536), jnp.float32)
    return pl.pallas_call(
        product_kernel,
        out_shape=(part,) * 4,
        in_specs=[SMEM] + [VMEM] * 6,
        out_specs=(VMEM,) * 4,
        scratch_shapes=[pltpu.VMEM((2, 8 * WIN, 256), jnp.float32)],
        compiler_params=pltpu.CompilerParams(vmem_limit_bytes=32 * 2**20),
        cost_estimate=pl.CostEstimate(flops=2 * 320 * 1536 * 512, bytes_accessed=4 * 2**20, transcendentals=0),
    )(at, w, *near, theirs)


def dot(left, right):
    return jnp.dot(left, right, preferred_element_type=jnp.float32).astype(jnp.bfloat16)


def shift(k):
    return [(i, (i + k) % 4) for i in range(4)]


def on_device(lower_block, solve_factor, schur_window):
    at = jnp.stack([lax.axis_index(n) for n in ("yhi", "ylo", "core", "x")])
    win = dot(lower_block[:WIN], solve_factor)
    w = jnp.broadcast_to(win[None], (8, WIN, 256))
    groups = [[(FIRST + 2 * i) % 16 + q for i in range(8)] for q in range(2)]
    w = lax.all_to_all(w, "z", 0, 0, tiled=True, axis_index_groups=groups)
    win, lower_block = lax.optimization_barrier((win, lower_block))
    panel = dot(lower_block, solve_factor)
    near = [
        panel,
        lax.ppermute(panel, "ylo", SWAP),
        lax.ppermute(panel, "yhi", SWAP),
        lax.ppermute(panel, ("ylo", "yhi"), [(i, 3 - i) for i in range(4)]),
    ]
    theirs = lax.ppermute(jnp.stack(near), "core", SWAP)
    w = jnp.roll(w, FIRST // 2, 0).reshape(1, 4, 2, WIN, 256).transpose(0, 2, 1, 3, 4)
    w = jnp.broadcast_to(w, (2, 2, 4, WIN, 256)).reshape(4, 4, WIN, 256)
    fours = [[z * 4 + i for i in range(4)] for z in range(8)]
    w = lax.all_to_all(w, ("z", "yhi"), 0, 0, tiled=True, axis_index_groups=fours)
    keep, *send = product(at, w, near, theirs)
    got = [lax.ppermute(send[k - 1], "x", shift(k)) for k in (2, 1, 3)]
    return schur_window - ((keep + got[1]) + (got[2] + got[0]))


def solution(mesh):
    fine = Mesh(mesh.devices.reshape(2, 2, 16, 4, 2), AXES)
    row, depth = ("ylo", "core"), ("x", "yhi")
    out = P(row + depth, "z")
    return jax.shard_map(
        on_device, mesh=fine, in_specs=(P(("z",) + row, None), P(None, depth), out), out_specs=out, check_vma=False
    )
```

time: 162 us -> 75.4 us (0.47)
  the two profiles are of different devices: /device:TPU:6 before, /device:TPU:10 now
where the time goes in v3:
time: 75.4 us; the launch traced here: 74.9 us
  starting transfers between devices  42.2 us (56%)
  waiting for transfers between devices  24.7 us (33%)
  local copies, waits for them, and re-layouts  2.68 us (4%)
  other arithmetic  2.05 us (3%)
  matrix products  1.75 us (2%)
  Pallas kernels  1.38 us (2%)
    ppermute x3, waiting for transfers between devices, on_device(): got = [lax.ppermute(send[k - 1], 'x', shift(k)) for k in (2, 1, 3)]  19.5 us
    all_to_all x1, starting transfers between devices, on_device(): w = lax.all_to_all(w, 'z', 0, 0, tiled=True, axis_index_groups=groups)  16.6 us
    ppermute x3, starting transfers between devices, on_device(): got = [lax.ppermute(send[k - 1], 'x', shift(k)) for k in (2, 1, 3)]  9.88 us
    all_to_all x1, starting transfers between devices, on_device(): lax.all_to_all(w, ('z', 'yhi'), 0, 0, tiled=True, axis_index_groups=fours)  4.02 us
    ppermute x1, starting transfers between devices, on_device(): lax.ppermute(panel, 'ylo', SWAP)  3.48 us
    ppermute x1, starting transfers between devices, on_device(): lax.ppermute(panel, ('ylo', 'yhi'), [(i, 3 - i) for i in range(4)])  3.48 us
    ppermute x1, starting transfers between devices, on_device(): lax.ppermute(panel, 'yhi', SWAP)  2.85 us
    ppermute x1, waiting for transfers between devices, on_device(): lax.ppermute(panel, 'ylo', SWAP)  2.72 us
  transfers between devices with their start and end apart: 9, of which 5 were waited for; matrix products, arithmetic and copies ran while one was open for 3% of the time, Pallas kernels for 0%

profile of v3, /device:TPU:10, one launch (start us, length us, event | category | flops | bytes accessed | tf_op | source)
XLA Modules:
  0.0 74.9 jit_solution(3673291253116020049)
XLA Ops:
  0.0 0.0 copy-start
  0.0 0.0 copy-start.2
  0.0 1.2 %copy-done = bf16[2048,256]{1,0:T(8,128)(2,1)S(1)} copy-done((bf16[2048,256]{1,0:T(8,128)(2,1)S(1)}, bf16[2048,256]{1,0:T(8,128)(2,1)}, u32[]{:S(2)}) %copy-start) | copy-done | bytes 1048600
  1.2 1.2 %convolution_convert_fusion.1 = bf16[40,256]{1,0:T(8,128)(2,1)S(1)} fusion(bf16[2048,256]{1,0:T(8,128)(2,1)S(1)} %copy-done, bf16[384,2048]{1,0:T(8,128)(2,1)} %param.3), kind=kOutput, calls=%fused_computation.1 | convolution fusion | flops 41953280 | bytes 1232896 | tf_op jit(solution)/shard_map/dot_general | solution.py:51
  2.4 0.7 broadcast_in_dim.6
  3.1 16.6 %all-to-all-start = ((bf16[8,40,256]{2,1,0:T(8,128)(2,1)}), bf16[8,40,256]{2,1,0:T(8,128)(2,1)S(1)}, u32[]{:S(2)}, u32[]{:S(2)}) async-start(bf16[8,40,256]{2,1,0:T(8,128)(2,1)} %broadcast_in_dim.6), calls=%async_computation | async-start | bytes 327680 | tf_op jit(solution)/shard_map/all_to_all | solution.py:63
  19.7 0.0 copy-done.2
  19.7 0.6 convolution_convert_fusion.n00
  20.3 3.5 %collective-permute-start.2 = (bf16[384,256]{1,0:T(8,128)(2,1)S(1)}, bf16[384,256]{1,0:T(8,128)(2,1)S(1)}, u32[]{:S(2)}, u32[]{:S(2)}) collective-permute-start(bf16[384,256]{1,0:T(8,128)(2,1)S(1)} %convolution_convert_fusion.n00), channel_id=1, source_target_pairs={{0,257},{1,256},{256,1},{257,0},{2,259},{3,258},{258,3},{259,2},{4... | collective-permute-start | bytes 589832 | tf_op jit(solution)/shard_map/ppermute | solution.py:70
  23.7 2.9 %collective-permute-start.1 = (bf16[384,256]{1,0:T(8,128)(2,1)S(1)}, bf16[384,256]{1,0:T(8,128)(2,1)S(1)}, u32[]{:S(2)}, u32[]{:S(2)}) collective-permute-start(bf16[384,256]{1,0:T(8,128)(2,1)S(1)} %convolution_convert_fusion.n00), channel_id=1, source_target_pairs={{0,1},{1,0},{2,3},{3,2},{4,5},{5,4},{6,7},{7,6},{8,9},{9,8},{10,11... | collective-permute-start | bytes 589832 | tf_op jit(solution)/shard_map/ppermute | solution.py:69
  26.6 3.5 %collective-permute-start = (bf16[384,256]{1,0:T(8,128)(2,1)S(1)}, bf16[384,256]{1,0:T(8,128)(2,1)S(1)}, u32[]{:S(2)}, u32[]{:S(2)}) collective-permute-start(bf16[384,256]{1,0:T(8,128)(2,1)S(1)} %convolution_convert_fusion.n00), channel_id=1, source_target_pairs={{0,256},{256,0},{1,257},{257,1},{2,258},{258,2},{3,259},{259,3},{4... | collective-permute-start | bytes 589832 | tf_op jit(solution)/shard_map/ppermute | solution.py:68
  30.1 0.0 all-to-all-done
  30.2 0.7 broadcast_in_dim.15
  30.9 4.0 %all-to-all-start.1 = ((bf16[4,4,40,256]{3,2,1,0:T(8,128)(2,1)}), bf16[4,4,40,256]{3,2,1,0:T(8,128)(2,1)S(1)}, u32[]{:S(2)}, u32[]{:S(2)}) async-start(bf16[4,4,40,256]{3,2,1,0:T(8,128)(2,1)} %bitcast.7), calls=%async_computation.1 | async-start | bytes 655360 | tf_op jit(solution)/shard_map/all_to_all | solution.py:76
  35.0 0.0 collective-permute-done.2.n11
  35.0 0.0 collective-permute-done.1.n10
  35.0 2.7 %collective-permute-done.n01 = bf16[384,256]{1,0:T(8,128)(2,1)S(1)} collective-permute-done((bf16[384,256]{1,0:T(8,128)(2,1)S(1)}, bf16[384,256]{1,0:T(8,128)(2,1)S(1)}, u32[]{:S(2)}, u32[]{:S(2)}) %collective-permute-start) | collective-permute-done | bytes 196640 | tf_op jit(solution)/shard_map/ppermute | solution.py:68
  37.7 0.0 copy-start.1
  37.7 1.0 %pad_maximum_fusion = bf16[4,384,256]{2,1,0:T(8,128)(2,1)} fusion(bf16[1,384,256]{2,1,0:T(8,128)(2,1)S(1)} %bitcast.18, bf16[1,384,256]{2,1,0:T(8,128)(2,1)S(1)} %bitcast.19, bf16[1,384,256]{2,1,0:T(8,128)(2,1)S(1)} %bitcast.20, bf16[1,384,256]{2,1,0:T(8,128)(2,1)S(1)} %bitcast.17), kind=kLoop, calls=%fused_computation.2 | loop fusion | flops 1179648 | bytes 1572864 | tf_op jit(solution)/shard_map/stack | solution.py:72
  38.7 1.9 %collective-permute-start.3 = (bf16[4,384,256]{2,1,0:T(8,128)(2,1)}, bf16[4,384,256]{2,1,0:T(8,128)(2,1)S(1)}, u32[]{:S(2)}, u32[]{:S(2)}) collective-permute-start(bf16[4,384,256]{2,1,0:T(8,128)(2,1)} %pad_maximum_fusion), channel_id=1, source_target_pairs={{0,128},{128,0},{1,129},{129,1},{2,130},{130,2},{3,131},{131,3},{4... | collective-permute-start | bytes 2359304 | tf_op jit(solution)/shard_map/ppermute | solution.py:72
  40.6 0.1 pad_add_fusion.at_ref
  40.7 2.4 %collective-permute-done.3.theirs = bf16[4,384,256]{2,1,0:T(8,128)(2,1)S(1)} collective-permute-done((bf16[4,384,256]{2,1,0:T(8,128)(2,1)}, bf16[4,384,256]{2,1,0:T(8,128)(2,1)S(1)}, u32[]{:S(2)}, u32[]{:S(2)}) %collective-permute-start.3) | collective-permute-done | bytes 786464 | tf_op jit(solution)/shard_map/ppermute | solution.py:72
  43.1 0.0 all-to-all-done.1.w
  43.1 1.4 %shard_map.37 = (f32[80,1536]{1,0:T(8,128)S(1)}, f32[80,1536]{1,0:T(8,128)S(1)}, f32[80,1536]{1,0:T(8,128)S(1)}, f32[80,1536]{1,0:T(8,128)S(1)}) custom-call(s32[4]{0:T(128)S(1)} %pad_add_fusion.at_ref, bf16[4,4,40,256]{3,2,1,0:T(8,128)(2,1)S(1)} %all-to-all-done.1.w, bf16[384,256]{1,0:T(8,128)(2,1)S(1)} %convolution_convert_fusion.n00, ...), custom_call_target="tpu_custom_call" | custom-call | flops 503316480 | bytes 4194304 | tf_op jit(solution)/shard_map/pallas_call | solution.py:39
  44.5 3.4 %collective-permute-start.4 = (f32[80,1536]{1,0:T(8,128)S(1)}, f32[80,1536]{1,0:T(8,128)S(1)}, u32[]{:S(2)}, u32[]{:S(2)}) collective-permute-start(f32[80,1536]{1,0:T(8,128)S(1)} %get-tuple-element.12), channel_id=1, source_target_pairs={{0,2},{2,4},{4,6},{6,0},{1,3},{3,5},{5,7},{7,1},{8,10},{10,12},{12... | collective-permute-start | bytes 1474568 | tf_op jit(solution)/shard_map/ppermute | solution.py:78
  47.9 2.4 %collective-permute-start.5 = (f32[80,1536]{1,0:T(8,128)S(1)}, f32[80,1536]{1,0:T(8,128)S(1)}, u32[]{:S(2)}, u32[]{:S(2)}) collective-permute-start(f32[80,1536]{1,0:T(8,128)S(1)} %get-tuple-element.13), channel_id=1, source_target_pairs={{0,6},{2,0},{4,2},{6,4},{1,7},{3,1},{5,3},{7,5},{8,14},{10,8},{12,... | collective-permute-start | bytes 1474568 | tf_op jit(solution)/shard_map/ppermute | solution.py:78
  50.3 4.0 %collective-permute-start.6 = (f32[80,1536]{1,0:T(8,128)S(1)}, f32[80,1536]{1,0:T(8,128)S(1)}, u32[]{:S(2)}, u32[]{:S(2)}) collective-permute-start(f32[80,1536]{1,0:T(8,128)S(1)} %get-tuple-element.14), channel_id=1, source_target_pairs={{0,4},{2,6},{4,0},{6,2},{1,5},{3,7},{5,1},{7,3},{8,12},{10,14},{12... | collective-permute-start | bytes 1474568 | tf_op jit(solution)/shard_map/ppermute | solution.py:78
  54.4 6.1 %collective-permute-done.4 = f32[80,1536]{1,0:T(8,128)S(1)} collective-permute-done((f32[80,1536]{1,0:T(8,128)S(1)}, f32[80,1536]{1,0:T(8,128)S(1)}, u32[]{:S(2)}, u32[]{:S(2)}) %collective-permute-start.4) | collective-permute-done | bytes 491552 | tf_op jit(solution)/shard_map/ppermute | solution.py:78
  60.4 2.8 %collective-permute-done.5 = f32[80,1536]{1,0:T(8,128)S(1)} collective-permute-done((f32[80,1536]{1,0:T(8,128)S(1)}, f32[80,1536]{1,0:T(8,128)S(1)}, u32[]{:S(2)}, u32[]{:S(2)}) %collective-permute-start.5) | collective-permute-done | bytes 491552 | tf_op jit(solution)/shard_map/ppermute | solution.py:78
  63.3 10.7 %collective-permute-done.6 = f32[80,1536]{1,0:T(8,128)S(1)} collective-permute-done((f32[80,1536]{1,0:T(8,128)S(1)}, f32[80,1536]{1,0:T(8,128)S(1)}, u32[]{:S(2)}, u32[]{:S(2)}) %collective-permute-start.6) | collective-permute-done | bytes 491552 | tf_op jit(solution)/shard_map/ppermute | solution.py:78
  73.9 0.0 copy-done.1
  73.9 0.9 %add_subtract_fusion = f32[80,1536]{1,0:T(8,128)} fusion(f32[80,1536]{1,0:T(8,128)S(1)} %copy-done.1, f32[80,1536]{1,0:T(8,128)S(1)} %collective-permute-done.5, f32[80,1536]{1,0:T(8,128)S(1)} %collective-permute-done.6, f32[80,1536]{1,0:T(8,128)S(1)} %get-tuple-element.11, f32[80,1536]{1,0:T(8,128)S(1)} %collective-permute-done.4), kind=kLoop, calls=%fused_computation.3 | loop fusion | flops 491520 | bytes 2949120 | tf_op jit(solution)/shard_map/sub | solution.py:79
  (4 shorter events, 0.0 us)
Async XLA Ops:
  0.0 1.2 %copy-start = (bf16[2048,256]{1,0:T(8,128)(2,1)S(1)}, bf16[2048,256]{1,0:T(8,128)(2,1)}, u32[]{:S(2)}) copy-start(bf16[2048,256]{1,0:T(8,128)(2,1)} %param.4) | copy-start | bytes 3145732
  0.0 19.7 %copy-start.2 = (bf16[384,2048]{1,0:T(8,128)(2,1)S(1)}, bf16[384,2048]{1,0:T(8,128)(2,1)}, u32[]{:S(2)}) copy-start(bf16[384,2048]{1,0:T(8,128)(2,1)} %param.3) | copy-start | bytes 4718596
  3.1 27.0 %all-to-all-start = ((bf16[8,40,256]{2,1,0:T(8,128)(2,1)}), bf16[8,40,256]{2,1,0:T(8,128)(2,1)S(1)}, u32[]{:S(2)}, u32[]{:S(2)}) async-start(bf16[8,40,256]{2,1,0:T(8,128)(2,1)} %broadcast_in_dim.6), calls=%async_computation | async-start | bytes 327680 | tf_op jit(solution)/shard_map/all_to_all | solution.py:63
  20.3 14.7 %collective-permute-start.2 = (bf16[384,256]{1,0:T(8,128)(2,1)S(1)}, bf16[384,256]{1,0:T(8,128)(2,1)S(1)}, u32[]{:S(2)}, u32[]{:S(2)}) collective-permute-start(bf16[384,256]{1,0:T(8,128)(2,1)S(1)} %convolution_convert_fusion.n00), channel_id=1, source_target_pairs={{0,257},{1,256},{256,1},{257,0},{2,259},{3,258},{258,3},{259,2},{4... | collective-permute-start | bytes 589832 | tf_op jit(solution)/shard_map/ppermute | solution.py:70
  23.7 11.2 %collective-permute-start.1 = (bf16[384,256]{1,0:T(8,128)(2,1)S(1)}, bf16[384,256]{1,0:T(8,128)(2,1)S(1)}, u32[]{:S(2)}, u32[]{:S(2)}) collective-permute-start(bf16[384,256]{1,0:T(8,128)(2,1)S(1)} %convolution_convert_fusion.n00), channel_id=1, source_target_pairs={{0,1},{1,0},{2,3},{3,2},{4,5},{5,4},{6,7},{7,6},{8,9},{9,8},{10,11... | collective-permute-start | bytes 589832 | tf_op jit(solution)/shard_map/ppermute | solution.py:69
  26.6 11.1 %collective-permute-start = (bf16[384,256]{1,0:T(8,128)(2,1)S(1)}, bf16[384,256]{1,0:T(8,128)(2,1)S(1)}, u32[]{:S(2)}, u32[]{:S(2)}) collective-permute-start(bf16[384,256]{1,0:T(8,128)(2,1)S(1)} %convolution_convert_fusion.n00), channel_id=1, source_target_pairs={{0,256},{256,0},{1,257},{257,1},{2,258},{258,2},{3,259},{259,3},{4... | collective-permute-start | bytes 589832 | tf_op jit(solution)/shard_map/ppermute | solution.py:68
  30.9 12.1 %all-to-all-start.1 = ((bf16[4,4,40,256]{3,2,1,0:T(8,128)(2,1)}), bf16[4,4,40,256]{3,2,1,0:T(8,128)(2,1)S(1)}, u32[]{:S(2)}, u32[]{:S(2)}) async-start(bf16[4,4,40,256]{3,2,1,0:T(8,128)(2,1)} %bitcast.7), calls=%async_computation.1 | async-start | bytes 655360 | tf_op jit(solution)/shard_map/all_to_all | solution.py:76
  37.7 36.2 %copy-start.1 = (f32[80,1536]{1,0:T(8,128)S(1)}, f32[80,1536]{1,0:T(8,128)}, u32[]{:S(2)}) copy-start(f32[80,1536]{1,0:T(8,128)} %param.5) | copy-start | bytes 1474564
  38.7 4.4 %collective-permute-start.3 = (bf16[4,384,256]{2,1,0:T(8,128)(2,1)}, bf16[4,384,256]{2,1,0:T(8,128)(2,1)S(1)}, u32[]{:S(2)}, u32[]{:S(2)}) collective-permute-start(bf16[4,384,256]{2,1,0:T(8,128)(2,1)} %pad_maximum_fusion), channel_id=1, source_target_pairs={{0,128},{128,0},{1,129},{129,1},{2,130},{130,2},{3,131},{131,3},{4... | collective-permute-start | bytes 2359304 | tf_op jit(solution)/shard_map/ppermute | solution.py:72
  44.5 16.0 %collective-permute-start.4 = (f32[80,1536]{1,0:T(8,128)S(1)}, f32[80,1536]{1,0:T(8,128)S(1)}, u32[]{:S(2)}, u32[]{:S(2)}) collective-permute-start(f32[80,1536]{1,0:T(8,128)S(1)} %get-tuple-element.12), channel_id=1, source_target_pairs={{0,2},{2,4},{4,6},{6,0},{1,3},{3,5},{5,7},{7,1},{8,10},{10,12},{12... | collective-permute-start | bytes 1474568 | tf_op jit(solution)/shard_map/ppermute | solution.py:78
  47.9 15.4 %collective-permute-start.5 = (f32[80,1536]{1,0:T(8,128)S(1)}, f32[80,1536]{1,0:T(8,128)S(1)}, u32[]{:S(2)}, u32[]{:S(2)}) collective-permute-start(f32[80,1536]{1,0:T(8,128)S(1)} %get-tuple-element.13), channel_id=1, source_target_pairs={{0,6},{2,0},{4,2},{6,4},{1,7},{3,1},{5,3},{7,5},{8,14},{10,8},{12,... | collective-permute-start | bytes 1474568 | tf_op jit(solution)/shard_map/ppermute | solution.py:78
  50.3 23.6 %collective-permute-start.6 = (f32[80,1536]{1,0:T(8,128)S(1)}, f32[80,1536]{1,0:T(8,128)S(1)}, u32[]{:S(2)}, u32[]{:S(2)}) collective-permute-start(f32[80,1536]{1,0:T(8,128)S(1)} %get-tuple-element.14), channel_id=1, source_target_pairs={{0,4},{2,6},{4,0},{6,2},{1,5},{3,7},{5,1},{7,3},{8,12},{10,14},{12... | collective-permute-start | bytes 1474568 | tf_op jit(solution)/shard_map/ppermute | solution.py:78

commit v4 on v3

--- a/solution.py
+++ b/solution.py
@@ -6,7 +6,7 @@
 from jax.sharding import Mesh, PartitionSpec as P
 
 AXES = ("ylo", "core", "z", "x", "yhi")
-FIRST = 10
+FIRST = 12
 WIN = 40
 SWAP = ((0, 1), (1, 0))
 VMEM = pl.BlockSpec(memory_space=pltpu.VMEM)
@@ -47,6 +47,25 @@
     )(at, w, *near, theirs)
 
 
+def window_kernel(lower, factor, out_ref):
+    rows = jnp.dot(lower[...], factor[...], preferred_element_type=jnp.float32)[:WIN].astype(jnp.bfloat16)
+    for i in range(8):
+        out_ref[i] = rows
+
+
+def window(lower_block, solve_factor):
+    inner, columns = solve_factor.shape
+    return pl.pallas_call(
+        window_kernel,
+        out_shape=jax.ShapeDtypeStruct((8, WIN, columns), jnp.bfloat16),
+        grid=(1,),
+        in_specs=[pl.BlockSpec((48, inner), lambda i: (0, 0)), pl.BlockSpec((inner, columns), lambda i: (0, 0))],
+        out_specs=pl.BlockSpec((8, WIN, columns), lambda i: (0, 0, 0)),
+        compiler_params=pltpu.CompilerParams(vmem_limit_bytes=60 * 2**20),
+        cost_estimate=pl.CostEstimate(flops=2 * 48 * inner * columns, bytes_accessed=2**20, transcendentals=0),
+    )(lower_block, solve_factor)
+
+
 def dot(left, right):
     return jnp.dot(left, right, preferred_element_type=jnp.float32).astype(jnp.bfloat16)
 
@@ -57,11 +76,10 @@
 
 def on_device(lower_block, solve_factor, schur_window):
     at = jnp.stack([lax.axis_index(n) for n in ("yhi", "ylo", "core", "x")])
-    win = dot(lower_block[:WIN], solve_factor)
-    w = jnp.broadcast_to(win[None], (8, WIN, 256))
+    w = window(lower_block, solve_factor)
+    w, lower_block = lax.optimization_barrier((w, lower_block))
     groups = [[(FIRST + 2 * i) % 16 + q for i in range(8)] for q in range(2)]
     w = lax.all_to_all(w, "z", 0, 0, tiled=True, axis_index_groups=groups)
-    win, lower_block = lax.optimization_barrier((win, lower_block))
     panel = dot(lower_block, solve_factor)
     near = [
         panel,

time: 75.4 us -> 73 us (0.968)
  the two profiles are of different devices: /device:TPU:10 before, /device:TPU:6 now
where the time goes in v4:
time: 73 us; the launch traced here: 71.8 us
  starting transfers between devices  41.6 us (57%)
  waiting for transfers between devices  23.8 us (33%)
  Pallas kernels  3.82 us (5%)
  other arithmetic  1.14 us (2%)
  local copies, waits for them, and re-layouts  0.79 us (1%)
    ppermute x3, waiting for transfers between devices, on_device(): got = [lax.ppermute(send[k - 1], 'x', shift(k)) for k in (2, 1, 3)]  17.2 us
    all_to_all x1, starting transfers between devices, on_device(): w = lax.all_to_all(w, 'z', 0, 0, tiled=True, axis_index_groups=groups)  15.6 us
    ppermute x3, starting transfers between devices, on_device(): got = [lax.ppermute(send[k - 1], 'x', shift(k)) for k in (2, 1, 3)]  9.15 us
    ppermute x1, starting transfers between devices, on_device(): lax.ppermute(panel, ('ylo', 'yhi'), [(i, 3 - i) for i in range(4)])  4.92 us
    all_to_all x1, starting transfers between devices, on_device(): lax.all_to_all(w, ('z', 'yhi'), 0, 0, tiled=True, axis_index_groups=fours)  4.9 us
    all_to_all x1, waiting for transfers between devices, on_device(): lax.all_to_all(w, ('z', 'yhi'), 0, 0, tiled=True, axis_index_groups=fours)  2.6 us
    ppermute x1, starting transfers between devices, on_device(): lax.ppermute(panel, 'yhi', SWAP)  2.54 us
    pallas_call x1, Pallas kernels, window(): pl.pallas_call(window_kernel, out_shape=jax.ShapeDtypeStruct((8, WIN, col...  2.43 us
  transfers between devices with their start and end apart: 9, of which 5 were waited for; matrix products, arithmetic and copies ran while one was open for 2% of the time, Pallas kernels for 0%

profile of v4, /device:TPU:6, one launch (start us, length us, event | category | flops | bytes accessed | tf_op | source)
XLA Modules:
  0.0 71.8 jit_solution(2999518364689079875)
XLA Ops:
  0.0 0.0 copy-start.1
  0.0 0.0 copy-start
  0.0 2.4 %shard_map.37 = bf16[8,40,256]{2,1,0:T(8,128)(2,1)} custom-call(bf16[384,2048]{1,0:T(8,128)(2,1)} %lower.1, bf16[2048,256]{1,0:T(8,128)(2,1)} %factor.1), custom_call_target="tpu_custom_call" | custom-call | flops 50331648 | bytes 1048576 | tf_op jit(solution)/shard_map/pallas_call | solution.py:58
  2.4 15.6 %all-to-all-start = ((bf16[8,40,256]{2,1,0:T(8,128)(2,1)}), bf16[8,40,256]{2,1,0:T(8,128)(2,1)S(1)}, u32[]{:S(2)}, u32[]{:S(2)}) async-start(bf16[8,40,256]{2,1,0:T(8,128)(2,1)} %shard_map.37), calls=%async_computation | async-start | bytes 327680 | tf_op jit(solution)/shard_map/all_to_all | solution.py:82
  18.1 0.0 copy-done.1
  18.1 0.0 copy-done
  18.1 0.6 convolution_convert_fusion.n00
  18.7 4.9 %collective-permute-start.2 = (bf16[384,256]{1,0:T(8,128)(2,1)S(1)}, bf16[384,256]{1,0:T(8,128)(2,1)S(1)}, u32[]{:S(2)}, u32[]{:S(2)}) collective-permute-start(bf16[384,256]{1,0:T(8,128)(2,1)S(1)} %convolution_convert_fusion.n00), channel_id=1, source_target_pairs={{0,257},{1,256},{256,1},{257,0},{2,259},{3,258},{258,3},{259,2},{4... | collective-permute-start | bytes 589832 | tf_op jit(solution)/shard_map/ppermute | solution.py:88
  23.6 2.5 %collective-permute-start.1 = (bf16[384,256]{1,0:T(8,128)(2,1)S(1)}, bf16[384,256]{1,0:T(8,128)(2,1)S(1)}, u32[]{:S(2)}, u32[]{:S(2)}) collective-permute-start(bf16[384,256]{1,0:T(8,128)(2,1)S(1)} %convolution_convert_fusion.n00), channel_id=1, source_target_pairs={{0,1},{1,0},{2,3},{3,2},{4,5},{5,4},{6,7},{7,6},{8,9},{9,8},{10,11... | collective-permute-start | bytes 589832 | tf_op jit(solution)/shard_map/ppermute | solution.py:87
  26.1 2.4 %collective-permute-start = (bf16[384,256]{1,0:T(8,128)(2,1)S(1)}, bf16[384,256]{1,0:T(8,128)(2,1)S(1)}, u32[]{:S(2)}, u32[]{:S(2)}) collective-permute-start(bf16[384,256]{1,0:T(8,128)(2,1)S(1)} %convolution_convert_fusion.n00), channel_id=1, source_target_pairs={{0,256},{256,0},{1,257},{257,1},{2,258},{258,2},{3,259},{259,3},{4... | collective-permute-start | bytes 589832 | tf_op jit(solution)/shard_map/ppermute | solution.py:86
  28.5 1.8 %all-to-all-done = bf16[8,40,256]{2,1,0:T(8,128)(2,1)S(1)} async-done(((bf16[8,40,256]{2,1,0:T(8,128)(2,1)}), bf16[8,40,256]{2,1,0:T(8,128)(2,1)S(1)}, u32[]{:S(2)}, u32[]{:S(2)}) %all-to-all-start) | async-done | bytes 163872 | tf_op jit(solution)/shard_map/all_to_all | solution.py:82
  30.4 0.7 %broadcast_in_dim.8 = bf16[2,2,4,40,256]{4,3,2,1,0:T(8,128)(2,1)} broadcast(bf16[2,4,40,256]{3,2,1,0:T(8,128)(2,1)S(1)} %copy.4), dimensions={1,2,3,4} | broadcast | bytes 491520 | tf_op jit(solution)/shard_map/broadcast_in_dim | solution.py:92
  31.1 4.9 %all-to-all-start.1 = ((bf16[4,4,40,256]{3,2,1,0:T(8,128)(2,1)}), bf16[4,4,40,256]{3,2,1,0:T(8,128)(2,1)S(1)}, u32[]{:S(2)}, u32[]{:S(2)}) async-start(bf16[4,4,40,256]{3,2,1,0:T(8,128)(2,1)} %bitcast.7), calls=%async_computation.1 | async-start | bytes 655360 | tf_op jit(solution)/shard_map/all_to_all | solution.py:94
  36.0 0.0 collective-permute-done.2.n11
  36.0 0.0 collective-permute-done.1.n10
  36.0 0.0 collective-permute-done.n01
  36.0 0.0 copy-start.2
  36.1 0.1 pad_maximum_fusion
  36.2 2.1 %collective-permute-start.3 = (bf16[4,384,256]{2,1,0:T(8,128)(2,1)S(1)}, bf16[4,384,256]{2,1,0:T(8,128)(2,1)S(1)}, u32[]{:S(2)}, u32[]{:S(2)}) collective-permute-start(bf16[4,384,256]{2,1,0:T(8,128)(2,1)S(1)} %pad_maximum_fusion), channel_id=1, source_target_pairs={{0,128},{128,0},{1,129},{129,1},{2,130},{130,2},{3,131},{131,3},{4... | collective-permute-start | bytes 2359304 | tf_op jit(solution)/shard_map/ppermute | solution.py:90
  38.2 0.1 pad_add_fusion.at_ref
  38.3 2.2 %collective-permute-done.3.theirs = bf16[4,384,256]{2,1,0:T(8,128)(2,1)S(1)} collective-permute-done((bf16[4,384,256]{2,1,0:T(8,128)(2,1)S(1)}, bf16[4,384,256]{2,1,0:T(8,128)(2,1)S(1)}, u32[]{:S(2)}, u32[]{:S(2)}) %collective-permute-start.3) | collective-permute-done | bytes 786464 | tf_op jit(solution)/shard_map/ppermute | solution.py:90
  40.5 2.6 %all-to-all-done.1.w = bf16[4,4,40,256]{3,2,1,0:T(8,128)(2,1)S(1)} async-done(((bf16[4,4,40,256]{3,2,1,0:T(8,128)(2,1)}), bf16[4,4,40,256]{3,2,1,0:T(8,128)(2,1)S(1)}, u32[]{:S(2)}, u32[]{:S(2)}) %all-to-all-start.1) | async-done | bytes 327712 | tf_op jit(solution)/shard_map/all_to_all | solution.py:94
  43.1 1.4 %shard_map.38 = (f32[80,1536]{1,0:T(8,128)S(1)}, f32[80,1536]{1,0:T(8,128)S(1)}, f32[80,1536]{1,0:T(8,128)S(1)}, f32[80,1536]{1,0:T(8,128)S(1)}) custom-call(s32[4]{0:T(128)S(1)} %pad_add_fusion.at_ref, bf16[4,4,40,256]{3,2,1,0:T(8,128)(2,1)S(1)} %all-to-all-done.1.w, bf16[384,256]{1,0:T(8,128)(2,1)S(1)} %convolution_convert_fusion.n00, ...), custom_call_target="tpu_custom_call" | custom-call | flops 503316480 | bytes 4194304 | tf_op jit(solution)/shard_map/pallas_call | solution.py:39
  44.5 2.4 %collective-permute-start.4 = (f32[80,1536]{1,0:T(8,128)S(1)}, f32[80,1536]{1,0:T(8,128)S(1)}, u32[]{:S(2)}, u32[]{:S(2)}) collective-permute-start(f32[80,1536]{1,0:T(8,128)S(1)} %get-tuple-element.14), channel_id=1, source_target_pairs={{0,2},{2,4},{4,6},{6,0},{1,3},{3,5},{5,7},{7,1},{8,10},{10,12},{12... | collective-permute-start | bytes 1474568 | tf_op jit(solution)/shard_map/ppermute | solution.py:96
  46.9 3.5 %collective-permute-start.5 = (f32[80,1536]{1,0:T(8,128)S(1)}, f32[80,1536]{1,0:T(8,128)S(1)}, u32[]{:S(2)}, u32[]{:S(2)}) collective-permute-start(f32[80,1536]{1,0:T(8,128)S(1)} %get-tuple-element.15), channel_id=1, source_target_pairs={{0,6},{2,0},{4,2},{6,4},{1,7},{3,1},{5,3},{7,5},{8,14},{10,8},{12,... | collective-permute-start | bytes 1474568 | tf_op jit(solution)/shard_map/ppermute | solution.py:96
  50.3 3.3 %collective-permute-start.6 = (f32[80,1536]{1,0:T(8,128)S(1)}, f32[80,1536]{1,0:T(8,128)S(1)}, u32[]{:S(2)}, u32[]{:S(2)}) collective-permute-start(f32[80,1536]{1,0:T(8,128)S(1)} %get-tuple-element.16), channel_id=1, source_target_pairs={{0,4},{2,6},{4,0},{6,2},{1,5},{3,7},{5,1},{7,3},{8,12},{10,14},{12... | collective-permute-start | bytes 1474568 | tf_op jit(solution)/shard_map/ppermute | solution.py:96
  53.6 6.9 %collective-permute-done.4 = f32[80,1536]{1,0:T(8,128)S(1)} collective-permute-done((f32[80,1536]{1,0:T(8,128)S(1)}, f32[80,1536]{1,0:T(8,128)S(1)}, u32[]{:S(2)}, u32[]{:S(2)}) %collective-permute-start.4) | collective-permute-done | bytes 491552 | tf_op jit(solution)/shard_map/ppermute | solution.py:96
  60.5 10.4 %collective-permute-done.5 = f32[80,1536]{1,0:T(8,128)S(1)} collective-permute-done((f32[80,1536]{1,0:T(8,128)S(1)}, f32[80,1536]{1,0:T(8,128)S(1)}, u32[]{:S(2)}, u32[]{:S(2)}) %collective-permute-start.5) | collective-permute-done | bytes 491552 | tf_op jit(solution)/shard_map/ppermute | solution.py:96
  70.9 0.0 collective-permute-done.6
  70.9 0.0 copy-done.2
  70.9 0.9 %add_subtract_fusion = f32[80,1536]{1,0:T(8,128)} fusion(f32[80,1536]{1,0:T(8,128)S(1)} %copy-done.2, f32[80,1536]{1,0:T(8,128)S(1)} %collective-permute-done.5, f32[80,1536]{1,0:T(8,128)S(1)} %collective-permute-done.6, f32[80,1536]{1,0:T(8,128)S(1)} %get-tuple-element.13, f32[80,1536]{1,0:T(8,128)S(1)} %collective-permute-done.4), kind=kLoop, calls=%fused_computation.2 | loop fusion | flops 491520 | bytes 2949120 | tf_op jit(solution)/shard_map/sub | solution.py:97
  (4 shorter events, 0.0 us)
Async XLA Ops:
  0.0 18.1 %copy-start.1 = (bf16[2048,256]{1,0:T(8,128)(2,1)S(1)}, bf16[2048,256]{1,0:T(8,128)(2,1)}, u32[]{:S(2)}) copy-start(bf16[2048,256]{1,0:T(8,128)(2,1)} %factor.1) | copy-start | bytes 3145732
  0.0 18.1 %copy-start = (bf16[384,2048]{1,0:T(8,128)(2,1)S(1)}, bf16[384,2048]{1,0:T(8,128)(2,1)}, u32[]{:S(2)}) copy-start(bf16[384,2048]{1,0:T(8,128)(2,1)} %lower.1) | copy-start | bytes 4718596
  2.4 27.9 %all-to-all-start = ((bf16[8,40,256]{2,1,0:T(8,128)(2,1)}), bf16[8,40,256]{2,1,0:T(8,128)(2,1)S(1)}, u32[]{:S(2)}, u32[]{:S(2)}) async-start(bf16[8,40,256]{2,1,0:T(8,128)(2,1)} %shard_map.37), calls=%async_computation | async-start | bytes 327680 | tf_op jit(solution)/shard_map/all_to_all | solution.py:82
  18.7 17.4 %collective-permute-start.2 = (bf16[384,256]{1,0:T(8,128)(2,1)S(1)}, bf16[384,256]{1,0:T(8,128)(2,1)S(1)}, u32[]{:S(2)}, u32[]{:S(2)}) collective-permute-start(bf16[384,256]{1,0:T(8,128)(2,1)S(1)} %convolution_convert_fusion.n00), channel_id=1, source_target_pairs={{0,257},{1,256},{256,1},{257,0},{2,259},{3,258},{258,3},{259,2},{4... | collective-permute-start | bytes 589832 | tf_op jit(solution)/shard_map/ppermute | solution.py:88
  23.6 12.4 %collective-permute-start.1 = (bf16[384,256]{1,0:T(8,128)(2,1)S(1)}, bf16[384,256]{1,0:T(8,128)(2,1)S(1)}, u32[]{:S(2)}, u32[]{:S(2)}) collective-permute-start(bf16[384,256]{1,0:T(8,128)(2,1)S(1)} %convolution_convert_fusion.n00), channel_id=1, source_target_pairs={{0,1},{1,0},{2,3},{3,2},{4,5},{5,4},{6,7},{7,6},{8,9},{9,8},{10,11... | collective-permute-start | bytes 589832 | tf_op jit(solution)/shard_map/ppermute | solution.py:87
  26.1 9.9 %collective-permute-start = (bf16[384,256]{1,0:T(8,128)(2,1)S(1)}, bf16[384,256]{1,0:T(8,128)(2,1)S(1)}, u32[]{:S(2)}, u32[]{:S(2)}) collective-permute-start(bf16[384,256]{1,0:T(8,128)(2,1)S(1)} %convolution_convert_fusion.n00), channel_id=1, source_target_pairs={{0,256},{256,0},{1,257},{257,1},{2,258},{258,2},{3,259},{259,3},{4... | collective-permute-start | bytes 589832 | tf_op jit(solution)/shard_map/ppermute | solution.py:86
  31.1 11.9 %all-to-all-start.1 = ((bf16[4,4,40,256]{3,2,1,0:T(8,128)(2,1)}), bf16[4,4,40,256]{3,2,1,0:T(8,128)(2,1)S(1)}, u32[]{:S(2)}, u32[]{:S(2)}) async-start(bf16[4,4,40,256]{3,2,1,0:T(8,128)(2,1)} %bitcast.7), calls=%async_computation.1 | async-start | bytes 655360 | tf_op jit(solution)/shard_map/all_to_all | solution.py:94
  36.0 34.8 %copy-start.2 = (f32[80,1536]{1,0:T(8,128)S(1)}, f32[80,1536]{1,0:T(8,128)}, u32[]{:S(2)}) copy-start(f32[80,1536]{1,0:T(8,128)} %param.5) | copy-start | bytes 1474564
  36.2 4.3 %collective-permute-start.3 = (bf16[4,384,256]{2,1,0:T(8,128)(2,1)S(1)}, bf16[4,384,256]{2,1,0:T(8,128)(2,1)S(1)}, u32[]{:S(2)}, u32[]{:S(2)}) collective-permute-start(bf16[4,384,256]{2,1,0:T(8,128)(2,1)S(1)} %pad_maximum_fusion), channel_id=1, source_target_pairs={{0,128},{128,0},{1,129},{129,1},{2,130},{130,2},{3,131},{131,3},{4... | collective-permute-start | bytes 2359304 | tf_op jit(solution)/shard_map/ppermute | solution.py:90
  44.5 16.1 %collective-permute-start.4 = (f32[80,1536]{1,0:T(8,128)S(1)}, f32[80,1536]{1,0:T(8,128)S(1)}, u32[]{:S(2)}, u32[]{:S(2)}) collective-permute-start(f32[80,1536]{1,0:T(8,128)S(1)} %get-tuple-element.14), channel_id=1, source_target_pairs={{0,2},{2,4},{4,6},{6,0},{1,3},{3,5},{5,7},{7,1},{8,10},{10,12},{12... | collective-permute-start | bytes 1474568 | tf_op jit(solution)/shard_map/ppermute | solution.py:96
  46.9 24.0 %collective-permute-start.5 = (f32[80,1536]{1,0:T(8,128)S(1)}, f32[80,1536]{1,0:T(8,128)S(1)}, u32[]{:S(2)}, u32[]{:S(2)}) collective-permute-start(f32[80,1536]{1,0:T(8,128)S(1)} %get-tuple-element.15), channel_id=1, source_target_pairs={{0,6},{2,0},{4,2},{6,4},{1,7},{3,1},{5,3},{7,5},{8,14},{10,8},{12,... | collective-permute-start | bytes 1474568 | tf_op jit(solution)/shard_map/ppermute | solution.py:96
  50.3 20.6 %collective-permute-start.6 = (f32[80,1536]{1,0:T(8,128)S(1)}, f32[80,1536]{1,0:T(8,128)S(1)}, u32[]{:S(2)}, u32[]{:S(2)}) collective-permute-start(f32[80,1536]{1,0:T(8,128)S(1)} %get-tuple-element.16), channel_id=1, source_target_pairs={{0,4},{2,6},{4,0},{6,2},{1,5},{3,7},{5,1},{7,3},{8,12},{10,14},{12... | collective-permute-start | bytes 1474568 | tf_op jit(solution)/shard_map/ppermute | solution.py:96

commit v5 on v4

--- a/solution.py
+++ b/solution.py
@@ -1,3 +1,5 @@
+import functools
+
 import jax
 import jax.numpy as jnp
 from jax import lax
@@ -13,8 +15,9 @@
 SMEM = pl.BlockSpec(memory_space=pltpu.SMEM)
 
 
-def product_kernel(at_ref, w, n00, n01, n10, n11, theirs, *refs):
-    outs, rows_ref = refs[:4], refs[4]
+def product_kernel(first, at_ref, w, *refs):
+    near = refs[:4] if first else [refs[0].at[i] for i in range(4)]
+    outs, rows_ref = refs[-5:-1], refs[-1]
     h, a, b, x = at_ref[0], at_ref[1], at_ref[2], at_ref[3]
     for dh in range(2):
         for k in range(4):
@@ -23,28 +26,28 @@
                 rows_ref[dh, start : start + WIN, :] = w[q * 2 + (h + dh) % 2, (x + k) % 4].astype(jnp.float32)
     left = [rows_ref[dh].astype(jnp.bfloat16) for dh in range(2)]
     for da in range(2):
-        for t in range(2):
-            total = None
-            for dh in range(2):
-                near = theirs[dh * 2 + da] if t else ((n00, n01), (n10, n11))[dh][da][...]
-                term = lax.dot_general(left[dh], near, (((1,), (1,)), ((), ())), preferred_element_type=jnp.float32)
-                total = term if total is None else total + term
-            cols = pl.multiple_of(((a + da) % 2) * 768 + ((b + t) % 2) * 384, 128)
-            for k in range(4):
-                outs[k][:, pl.ds(cols, 384)] = total[k * 2 * WIN : (k + 1) * 2 * WIN]
+        total = None
+        for dh in range(2):
+            term = lax.dot_general(left[dh], near[dh * 2 + da][...], (((1,), (1,)), ((), ())), preferred_element_type=jnp.float32)
+            total = term if total is None else total + term
+        cols = pl.multiple_of(((a + da) % 2) * 768 + ((b + (0 if first else 1)) % 2) * 384, 128)
+        for k in range(4):
+            outs[k][:, pl.ds(cols, 384)] = total[k * 2 * WIN : (k + 1) * 2 * WIN]
 
 
-def product(at, w, near, theirs):
+def product(at, w, near, into=()):
     part = jax.ShapeDtypeStruct((2 * WIN, 1536), jnp.float32)
+    first = not into
     return pl.pallas_call(
-        product_kernel,
+        functools.partial(product_kernel, first),
         out_shape=(part,) * 4,
-        in_specs=[SMEM] + [VMEM] * 6,
+        in_specs=[SMEM] + [VMEM] * (1 + len(near) + len(into)),
         out_specs=(VMEM,) * 4,
         scratch_shapes=[pltpu.VMEM((2, 8 * WIN, 256), jnp.float32)],
+        input_output_aliases={2 + len(near) + i: i for i in range(len(into))},
         compiler_params=pltpu.CompilerParams(vmem_limit_bytes=32 * 2**20),
-        cost_estimate=pl.CostEstimate(flops=2 * 320 * 1536 * 512, bytes_accessed=4 * 2**20, transcendentals=0),
-    )(at, w, *near, theirs)
+        cost_estimate=pl.CostEstimate(flops=2 * 320 * 768 * 512, bytes_accessed=2 * 2**20, transcendentals=0),
+    )(at, w, *near, *into)
 
 
 def window_kernel(lower, factor, out_ref):
@@ -78,7 +81,7 @@
     at = jnp.stack([lax.axis_index(n) for n in ("yhi", "ylo", "core", "x")])
     w = window(lower_block, solve_factor)
     w, lower_block = lax.optimization_barrier((w, lower_block))
-    groups = [[(FIRST + 2 * i) % 16 + q for i in range(8)] for q in range(2)]
+    groups = [[(FIRST + 4 * i + 2 * h) % 16 + q for h in range(2) for i in range(4)] for q in range(2)]
     w = lax.all_to_all(w, "z", 0, 0, tiled=True, axis_index_groups=groups)
     panel = dot(lower_block, solve_factor)
     near = [
@@ -88,11 +91,11 @@
         lax.ppermute(panel, ("ylo", "yhi"), [(i, 3 - i) for i in range(4)]),
     ]
     theirs = lax.ppermute(jnp.stack(near), "core", SWAP)
-    w = jnp.roll(w, FIRST // 2, 0).reshape(1, 4, 2, WIN, 256).transpose(0, 2, 1, 3, 4)
-    w = jnp.broadcast_to(w, (2, 2, 4, WIN, 256)).reshape(4, 4, WIN, 256)
+    w = jnp.roll(w.reshape(2, 4, WIN, 256), FIRST // 4, 1)
+    w = jnp.broadcast_to(w[None], (2, 2, 4, WIN, 256)).reshape(4, 4, WIN, 256)
     fours = [[z * 4 + i for i in range(4)] for z in range(8)]
     w = lax.all_to_all(w, ("z", "yhi"), 0, 0, tiled=True, axis_index_groups=fours)
-    keep, *send = product(at, w, near, theirs)
+    keep, *send = product(at, w, [theirs], product(at, w, near))
     got = [lax.ppermute(send[k - 1], "x", shift(k)) for k in (2, 1, 3)]
     return schur_window - ((keep + got[1]) + (got[2] + got[0]))
 

time: 73 us -> 72.3 us (level)
  waiting for transfers between devices: 23.8 us -> 21.1 us
  starting transfers between devices: 41.6 us -> 42.6 us
    all_to_all x1, waiting for transfers between devices: 2.6 us -> 4.91 us  [on_device(): lax.all_to_all(w, ('z', 'yhi'), 0, 0, tiled=True, axis_index_groups=fours)]
    ppermute x1, waiting for transfers between devices: 2.17 us -> 0.01 us  [on_device(): theirs = lax.ppermute(jnp.stack(near), 'core', SWAP)]
    all_to_all x1, waiting for transfers between devices: 1.8 us -> 0.15 us  [on_device(): w = lax.all_to_all(w, 'z', 0, 0, tiled=True, axis_index_groups=groups)]
    ppermute x3, waiting for transfers between devices: 17.2 us -> 16 us  [on_device(): got = [lax.ppermute(send[k - 1], 'x', shift(k)) for k in (2, 1, 3)]]
    all_to_all x1, starting transfers between devices: 4.9 us -> 6.08 us  [on_device(): lax.all_to_all(w, ('z', 'yhi'), 0, 0, tiled=True, axis_index_groups=fours)]
    pallas_call x1 -> x2, Pallas kernels: 1.39 us -> 2.09 us  [product(): pl.pallas_call(functools.partial(product_kernel, first), out_shape=(part,...]
  transfers between devices with their start and end apart: 9 -> 9, of which waited for: 5 -> 4; matrix products, arithmetic and copies ran while one was open for 2% -> 2% of each run, Pallas kernels for 0% -> 1%
where the time goes in v5:
time: 72.3 us; the launch traced here: 70.9 us
  starting transfers between devices  42.6 us (59%)
  waiting for transfers between devices  21.1 us (29%)
  Pallas kernels  4.52 us (6%)
  other arithmetic  1.14 us (2%)
  local copies, waits for them, and re-layouts  0.77 us (1%)
    ppermute x3, waiting for transfers between devices, on_device(): got = [lax.ppermute(send[k - 1], 'x', shift(k)) for k in (2, 1, 3)]  16 us
    all_to_all x1, starting transfers between devices, on_device(): w = lax.all_to_all(w, 'z', 0, 0, tiled=True, axis_index_groups=groups)  15.6 us
    ppermute x3, starting transfers between devices, on_device(): got = [lax.ppermute(send[k - 1], 'x', shift(k)) for k in (2, 1, 3)]  9.15 us
    all_to_all x1, starting transfers between devices, on_device(): lax.all_to_all(w, ('z', 'yhi'), 0, 0, tiled=True, axis_index_groups=fours)  6.08 us
    ppermute x1, starting transfers between devices, on_device(): lax.ppermute(panel, ('ylo', 'yhi'), [(i, 3 - i) for i in range(4)])  4.92 us
    all_to_all x1, waiting for transfers between devices, on_device(): lax.all_to_all(w, ('z', 'yhi'), 0, 0, tiled=True, axis_index_groups=fours)  4.91 us
    ppermute x1, starting transfers between devices, on_device(): lax.ppermute(panel, 'yhi', SWAP)  2.54 us
    pallas_call x1, Pallas kernels, window(): pl.pallas_call(window_kernel, out_shape=jax.ShapeDtypeStruct((8, WIN, col...  2.43 us
  transfers between devices with their start and end apart: 9, of which 4 were waited for; matrix products, arithmetic and copies ran while one was open for 2% of the time, Pallas kernels for 1%

profile of v5, /device:TPU:6, one launch (start us, length us, event | category | flops | bytes accessed | tf_op | source)
XLA Modules:
  0.0 70.9 jit_solution(7089853577121912227)
XLA Ops:
  0.0 0.0 copy-start.1
  0.0 0.0 copy-start
  0.0 2.4 %shard_map.37 = bf16[8,40,256]{2,1,0:T(8,128)(2,1)} custom-call(bf16[384,2048]{1,0:T(8,128)(2,1)} %lower.1, bf16[2048,256]{1,0:T(8,128)(2,1)} %factor.1), custom_call_target="tpu_custom_call" | custom-call | flops 50331648 | bytes 1048576 | tf_op jit(solution)/shard_map/pallas_call | solution.py:61
  2.4 15.6 %all-to-all-start = ((bf16[8,40,256]{2,1,0:T(8,128)(2,1)}), bf16[8,40,256]{2,1,0:T(8,128)(2,1)S(1)}, u32[]{:S(2)}, u32[]{:S(2)}) async-start(bf16[8,40,256]{2,1,0:T(8,128)(2,1)} %shard_map.37), calls=%async_computation | async-start | bytes 327680 | tf_op jit(solution)/shard_map/all_to_all | solution.py:85
  18.1 0.0 copy-done.1
  18.1 0.0 copy-done
  18.1 0.6 convolution_convert_fusion.refs_0_
  18.7 4.9 %collective-permute-start.2 = (bf16[384,256]{1,0:T(8,128)(2,1)S(1)}, bf16[384,256]{1,0:T(8,128)(2,1)S(1)}, u32[]{:S(2)}, u32[]{:S(2)}) collective-permute-start(bf16[384,256]{1,0:T(8,128)(2,1)S(1)} %convolution_convert_fusion.refs_0_), channel_id=1, source_target_pairs={{0,257},{1,256},{256,1},{257,0},{2,259},{3,258},{258,3},{259,2},{4... | collective-permute-start | bytes 589832 | tf_op jit(solution)/shard_map/ppermute | solution.py:91
  23.6 2.5 %collective-permute-start.1 = (bf16[384,256]{1,0:T(8,128)(2,1)S(1)}, bf16[384,256]{1,0:T(8,128)(2,1)S(1)}, u32[]{:S(2)}, u32[]{:S(2)}) collective-permute-start(bf16[384,256]{1,0:T(8,128)(2,1)S(1)} %convolution_convert_fusion.refs_0_), channel_id=1, source_target_pairs={{0,1},{1,0},{2,3},{3,2},{4,5},{5,4},{6,7},{7,6},{8,9},{9,8},{10,11... | collective-permute-start | bytes 589832 | tf_op jit(solution)/shard_map/ppermute | solution.py:90
  26.1 2.4 %collective-permute-start = (bf16[384,256]{1,0:T(8,128)(2,1)S(1)}, bf16[384,256]{1,0:T(8,128)(2,1)S(1)}, u32[]{:S(2)}, u32[]{:S(2)}) collective-permute-start(bf16[384,256]{1,0:T(8,128)(2,1)S(1)} %convolution_convert_fusion.refs_0_), channel_id=1, source_target_pairs={{0,256},{256,0},{1,257},{257,1},{2,258},{258,2},{3,259},{259,3},{4... | collective-permute-start | bytes 589832 | tf_op jit(solution)/shard_map/ppermute | solution.py:89
  28.5 0.2 all-to-all-done
  28.7 0.7 %broadcast_in_dim.2 = bf16[2,2,4,40,256]{4,3,2,1,0:T(8,128)(2,1)} broadcast(bf16[2,4,40,256]{3,2,1,0:T(8,128)(2,1)S(1)} %pad_maximum_fusion.1), dimensions={1,2,3,4} | broadcast | bytes 491520 | tf_op jit(solution)/shard_map/broadcast_in_dim | solution.py:95
  29.5 6.1 %all-to-all-start.1 = ((bf16[4,4,40,256]{3,2,1,0:T(8,128)(2,1)}), bf16[4,4,40,256]{3,2,1,0:T(8,128)(2,1)S(1)}, u32[]{:S(2)}, u32[]{:S(2)}) async-start(bf16[4,4,40,256]{3,2,1,0:T(8,128)(2,1)} %bitcast.5), calls=%async_computation.1 | async-start | bytes 655360 | tf_op jit(solution)/shard_map/all_to_all | solution.py:97
  35.5 0.0 collective-permute-done.2.refs_3_
  35.5 0.0 collective-permute-done.1.refs_2_
  35.5 0.0 collective-permute-done.refs_1_
  35.6 0.1 pad_maximum_fusion
  35.7 1.9 %collective-permute-start.3 = (bf16[4,384,256]{2,1,0:T(8,128)(2,1)S(1)}, bf16[4,384,256]{2,1,0:T(8,128)(2,1)S(1)}, u32[]{:S(2)}, u32[]{:S(2)}) collective-permute-start(bf16[4,384,256]{2,1,0:T(8,128)(2,1)S(1)} %pad_maximum_fusion), channel_id=1, source_target_pairs={{0,128},{128,0},{1,129},{129,1},{2,130},{130,2},{3,131},{131,3},{4... | collective-permute-start | bytes 2359304 | tf_op jit(solution)/shard_map/ppermute | solution.py:93
  37.6 0.1 pad_add_fusion.at_ref
  37.7 4.9 %all-to-all-done.1.w = bf16[4,4,40,256]{3,2,1,0:T(8,128)(2,1)S(1)} async-done(((bf16[4,4,40,256]{3,2,1,0:T(8,128)(2,1)}), bf16[4,4,40,256]{3,2,1,0:T(8,128)(2,1)S(1)}, u32[]{:S(2)}, u32[]{:S(2)}) %all-to-all-start.1) | async-done | bytes 327712 | tf_op jit(solution)/shard_map/all_to_all | solution.py:97
  42.6 1.0 %shard_map.38 = (f32[80,1536]{1,0:T(8,128)S(1)}, f32[80,1536]{1,0:T(8,128)S(1)}, f32[80,1536]{1,0:T(8,128)S(1)}, f32[80,1536]{1,0:T(8,128)S(1)}) custom-call(s32[4]{0:T(128)S(1)} %pad_add_fusion.at_ref, bf16[4,4,40,256]{3,2,1,0:T(8,128)(2,1)S(1)} %all-to-all-done.1.w, bf16[384,256]{1,0:T(8,128)(2,1)S(1)} %convolution_convert_fusion.refs_0_, ...), custom_call_target="tpu_custom_call" | custom-call | flops 251658240 | bytes 2097152 | tf_op jit(solution)/shard_map/pallas_call | solution.py:41
  43.6 0.0 copy-start.2
  43.7 0.0 collective-permute-done.3.refs_0_
  43.7 1.0 %shard_map.39 = (f32[80,1536]{1,0:T(8,128)S(1)}, f32[80,1536]{1,0:T(8,128)S(1)}, f32[80,1536]{1,0:T(8,128)S(1)}, f32[80,1536]{1,0:T(8,128)S(1)}) custom-call(s32[4]{0:T(128)S(1)} %pad_add_fusion.at_ref, bf16[4,4,40,256]{3,2,1,0:T(8,128)(2,1)S(1)} %all-to-all-done.1.w, ...), custom_call_target="tpu_custom_call", output_to_operand_aliasing={{0}: (3, {}), {1}: (4, {}), {2}: (5, {}), {3}: (6, {})} | custom-call | flops 251658240 | bytes 2097152 | tf_op jit(solution)/shard_map/pallas_call | solution.py:41
  44.7 2.4 %collective-permute-start.4 = (f32[80,1536]{1,0:T(8,128)S(1)}, f32[80,1536]{1,0:T(8,128)S(1)}, u32[]{:S(2)}, u32[]{:S(2)}) collective-permute-start(f32[80,1536]{1,0:T(8,128)S(1)} %get-tuple-element.22), channel_id=1, source_target_pairs={{0,2},{2,4},{4,6},{6,0},{1,3},{3,5},{5,7},{7,1},{8,10},{10,12},{12... | collective-permute-start | bytes 1474568 | tf_op jit(solution)/shard_map/ppermute | solution.py:99
  47.1 3.5 %collective-permute-start.5 = (f32[80,1536]{1,0:T(8,128)S(1)}, f32[80,1536]{1,0:T(8,128)S(1)}, u32[]{:S(2)}, u32[]{:S(2)}) collective-permute-start(f32[80,1536]{1,0:T(8,128)S(1)} %get-tuple-element.23), channel_id=1, source_target_pairs={{0,6},{2,0},{4,2},{6,4},{1,7},{3,1},{5,3},{7,5},{8,14},{10,8},{12,... | collective-permute-start | bytes 1474568 | tf_op jit(solution)/shard_map/ppermute | solution.py:99
  50.6 3.3 %collective-permute-start.6 = (f32[80,1536]{1,0:T(8,128)S(1)}, f32[80,1536]{1,0:T(8,128)S(1)}, u32[]{:S(2)}, u32[]{:S(2)}) collective-permute-start(f32[80,1536]{1,0:T(8,128)S(1)} %get-tuple-element.24), channel_id=1, source_target_pairs={{0,4},{2,6},{4,0},{6,2},{1,5},{3,7},{5,1},{7,3},{8,12},{10,14},{12... | collective-permute-start | bytes 1474568 | tf_op jit(solution)/shard_map/ppermute | solution.py:99
  53.9 6.8 %collective-permute-done.4 = f32[80,1536]{1,0:T(8,128)S(1)} collective-permute-done((f32[80,1536]{1,0:T(8,128)S(1)}, f32[80,1536]{1,0:T(8,128)S(1)}, u32[]{:S(2)}, u32[]{:S(2)}) %collective-permute-start.4) | collective-permute-done | bytes 491552 | tf_op jit(solution)/shard_map/ppermute | solution.py:99
  60.7 9.2 %collective-permute-done.5 = f32[80,1536]{1,0:T(8,128)S(1)} collective-permute-done((f32[80,1536]{1,0:T(8,128)S(1)}, f32[80,1536]{1,0:T(8,128)S(1)}, u32[]{:S(2)}, u32[]{:S(2)}) %collective-permute-start.5) | collective-permute-done | bytes 491552 | tf_op jit(solution)/shard_map/ppermute | solution.py:99
  69.9 0.0 collective-permute-done.6
  69.9 0.0 copy-done.2
  69.9 0.9 %add_subtract_fusion = f32[80,1536]{1,0:T(8,128)} fusion(f32[80,1536]{1,0:T(8,128)S(1)} %copy-done.2, f32[80,1536]{1,0:T(8,128)S(1)} %collective-permute-done.5, f32[80,1536]{1,0:T(8,128)S(1)} %collective-permute-done.6, f32[80,1536]{1,0:T(8,128)S(1)} %get-tuple-element.21, f32[80,1536]{1,0:T(8,128)S(1)} %collective-permute-done.4), kind=kLoop, calls=%fused_computation.2 | loop fusion | flops 491520 | bytes 2949120 | tf_op jit(solution)/shard_map/sub | solution.py:100
  (3 shorter events, 0.0 us)
Async XLA Ops:
  0.0 18.1 %copy-start.1 = (bf16[2048,256]{1,0:T(8,128)(2,1)S(1)}, bf16[2048,256]{1,0:T(8,128)(2,1)}, u32[]{:S(2)}) copy-start(bf16[2048,256]{1,0:T(8,128)(2,1)} %factor.1) | copy-start | bytes 3145732
  0.0 18.1 %copy-start = (bf16[384,2048]{1,0:T(8,128)(2,1)S(1)}, bf16[384,2048]{1,0:T(8,128)(2,1)}, u32[]{:S(2)}) copy-start(bf16[384,2048]{1,0:T(8,128)(2,1)} %lower.1) | copy-start | bytes 4718596
  2.4 26.2 %all-to-all-start = ((bf16[8,40,256]{2,1,0:T(8,128)(2,1)}), bf16[8,40,256]{2,1,0:T(8,128)(2,1)S(1)}, u32[]{:S(2)}, u32[]{:S(2)}) async-start(bf16[8,40,256]{2,1,0:T(8,128)(2,1)} %shard_map.37), calls=%async_computation | async-start | bytes 327680 | tf_op jit(solution)/shard_map/all_to_all | solution.py:85
  18.7 16.9 %collective-permute-start.2 = (bf16[384,256]{1,0:T(8,128)(2,1)S(1)}, bf16[384,256]{1,0:T(8,128)(2,1)S(1)}, u32[]{:S(2)}, u32[]{:S(2)}) collective-permute-start(bf16[384,256]{1,0:T(8,128)(2,1)S(1)} %convolution_convert_fusion.refs_0_), channel_id=1, source_target_pairs={{0,257},{1,256},{256,1},{257,0},{2,259},{3,258},{258,3},{259,2},{4... | collective-permute-start | bytes 589832 | tf_op jit(solution)/shard_map/ppermute | solution.py:91
  23.6 11.9 %collective-permute-start.1 = (bf16[384,256]{1,0:T(8,128)(2,1)S(1)}, bf16[384,256]{1,0:T(8,128)(2,1)S(1)}, u32[]{:S(2)}, u32[]{:S(2)}) collective-permute-start(bf16[384,256]{1,0:T(8,128)(2,1)S(1)} %convolution_convert_fusion.refs_0_), channel_id=1, source_target_pairs={{0,1},{1,0},{2,3},{3,2},{4,5},{5,4},{6,7},{7,6},{8,9},{9,8},{10,11... | collective-permute-start | bytes 589832 | tf_op jit(solution)/shard_map/ppermute | solution.py:90
  26.1 9.4 %collective-permute-start = (bf16[384,256]{1,0:T(8,128)(2,1)S(1)}, bf16[384,256]{1,0:T(8,128)(2,1)S(1)}, u32[]{:S(2)}, u32[]{:S(2)}) collective-permute-start(bf16[384,256]{1,0:T(8,128)(2,1)S(1)} %convolution_convert_fusion.refs_0_), channel_id=1, source_target_pairs={{0,256},{256,0},{1,257},{257,1},{2,258},{258,2},{3,259},{259,3},{4... | collective-permute-start | bytes 589832 | tf_op jit(solution)/shard_map/ppermute | solution.py:89
  29.5 13.1 %all-to-all-start.1 = ((bf16[4,4,40,256]{3,2,1,0:T(8,128)(2,1)}), bf16[4,4,40,256]{3,2,1,0:T(8,128)(2,1)S(1)}, u32[]{:S(2)}, u32[]{:S(2)}) async-start(bf16[4,4,40,256]{3,2,1,0:T(8,128)(2,1)} %bitcast.5), calls=%async_computation.1 | async-start | bytes 655360 | tf_op jit(solution)/shard_map/all_to_all | solution.py:97
  35.7 8.0 %collective-permute-start.3 = (bf16[4,384,256]{2,1,0:T(8,128)(2,1)S(1)}, bf16[4,384,256]{2,1,0:T(8,128)(2,1)S(1)}, u32[]{:S(2)}, u32[]{:S(2)}) collective-permute-start(bf16[4,384,256]{2,1,0:T(8,128)(2,1)S(1)} %pad_maximum_fusion), channel_id=1, source_target_pairs={{0,128},{128,0},{1,129},{129,1},{2,130},{130,2},{3,131},{131,3},{4... | collective-permute-start | bytes 2359304 | tf_op jit(solution)/shard_map/ppermute | solution.py:93
  43.6 26.3 %copy-start.2 = (f32[80,1536]{1,0:T(8,128)S(1)}, f32[80,1536]{1,0:T(8,128)}, u32[]{:S(2)}) copy-start(f32[80,1536]{1,0:T(8,128)} %param.5) | copy-start | bytes 1474564
  44.7 16.0 %collective-permute-start.4 = (f32[80,1536]{1,0:T(8,128)S(1)}, f32[80,1536]{1,0:T(8,128)S(1)}, u32[]{:S(2)}, u32[]{:S(2)}) collective-permute-start(f32[80,1536]{1,0:T(8,128)S(1)} %get-tuple-element.22), channel_id=1, source_target_pairs={{0,2},{2,4},{4,6},{6,0},{1,3},{3,5},{5,7},{7,1},{8,10},{10,12},{12... | collective-permute-start | bytes 1474568 | tf_op jit(solution)/shard_map/ppermute | solution.py:99
  47.1 22.8 %collective-permute-start.5 = (f32[80,1536]{1,0:T(8,128)S(1)}, f32[80,1536]{1,0:T(8,128)S(1)}, u32[]{:S(2)}, u32[]{:S(2)}) collective-permute-start(f32[80,1536]{1,0:T(8,128)S(1)} %get-tuple-element.23), channel_id=1, source_target_pairs={{0,6},{2,0},{4,2},{6,4},{1,7},{3,1},{5,3},{7,5},{8,14},{10,8},{12,... | collective-permute-start | bytes 1474568 | tf_op jit(solution)/shard_map/ppermute | solution.py:99
  50.6 19.3 %collective-permute-start.6 = (f32[80,1536]{1,0:T(8,128)S(1)}, f32[80,1536]{1,0:T(8,128)S(1)}, u32[]{:S(2)}, u32[]{:S(2)}) collective-permute-start(f32[80,1536]{1,0:T(8,128)S(1)} %get-tuple-element.24), channel_id=1, source_target_pairs={{0,4},{2,6},{4,0},{6,2},{1,5},{3,7},{5,1},{7,3},{8,12},{10,14},{12... | collective-permute-start | bytes 1474568 | tf_op jit(solution)/shard_map/ppermute | solution.py:99

commit v6 on v5

--- a/solution.py
+++ b/solution.py
@@ -30,21 +30,26 @@
         for dh in range(2):
             term = lax.dot_general(left[dh], near[dh * 2 + da][...], (((1,), (1,)), ((), ())), preferred_element_type=jnp.float32)
             total = term if total is None else total + term
-        cols = pl.multiple_of(((a + da) % 2) * 768 + ((b + (0 if first else 1)) % 2) * 384, 128)
+        where = (a + da) % 2
+        cols = where * 384 if first else where * 768 + (1 - b) * 384
         for k in range(4):
-            outs[k][:, pl.ds(cols, 384)] = total[k * 2 * WIN : (k + 1) * 2 * WIN]
+            outs[k][:, pl.ds(pl.multiple_of(cols, 128), 384)] = total[k * 2 * WIN : (k + 1) * 2 * WIN]
+    if not first:
+        for k in range(4):
+            for y in range(2):
+                cols = pl.ds(pl.multiple_of(y * 768 + b * 384, 128), 384)
+                outs[k][:, cols] = refs[1 + k][:, y * 384 : (y + 1) * 384]
 
 
 def product(at, w, near, into=()):
-    part = jax.ShapeDtypeStruct((2 * WIN, 1536), jnp.float32)
     first = not into
+    part = jax.ShapeDtypeStruct((2 * WIN, 768 if first else 1536), jnp.float32)
     return pl.pallas_call(
         functools.partial(product_kernel, first),
         out_shape=(part,) * 4,
         in_specs=[SMEM] + [VMEM] * (1 + len(near) + len(into)),
         out_specs=(VMEM,) * 4,
         scratch_shapes=[pltpu.VMEM((2, 8 * WIN, 256), jnp.float32)],
-        input_output_aliases={2 + len(near) + i: i for i in range(len(into))},
         compiler_params=pltpu.CompilerParams(vmem_limit_bytes=32 * 2**20),
         cost_estimate=pl.CostEstimate(flops=2 * 320 * 768 * 512, bytes_accessed=2 * 2**20, transcendentals=0),
     )(at, w, *near, *into)

time: 72.3 us -> 72.3 us (level)
  no operation moved by 1% of the time
where the time goes in v6:
time: 72.3 us; the launch traced here: 70.9 us
  starting transfers between devices  42.6 us (59%)
  waiting for transfers between devices  21.1 us (29%)
  Pallas kernels  4.56 us (6%)
  other arithmetic  1.17 us (2%)
  local copies, waits for them, and re-layouts  0.77 us (1%)
    ppermute x3, waiting for transfers between devices, on_device(): got = [lax.ppermute(send[k - 1], 'x', shift(k)) for k in (2, 1, 3)]  16 us
    all_to_all x1, starting transfers between devices, on_device(): w = lax.all_to_all(w, 'z', 0, 0, tiled=True, axis_index_groups=groups)  15.6 us
    ppermute x3, starting transfers between devices, on_device(): got = [lax.ppermute(send[k - 1], 'x', shift(k)) for k in (2, 1, 3)]  9.15 us
    all_to_all x1, starting transfers between devices, on_device(): lax.all_to_all(w, ('z', 'yhi'), 0, 0, tiled=True, axis_index_groups=fours)  6.08 us
    ppermute x1, starting transfers between devices, on_device(): lax.ppermute(panel, ('ylo', 'yhi'), [(i, 3 - i) for i in range(4)])  4.92 us
    all_to_all x1, waiting for transfers between devices, on_device(): lax.all_to_all(w, ('z', 'yhi'), 0, 0, tiled=True, axis_index_groups=fours)  4.91 us
    ppermute x1, starting transfers between devices, on_device(): lax.ppermute(panel, 'yhi', SWAP)  2.54 us
    pallas_call x1, Pallas kernels, window(): pl.pallas_call(window_kernel, out_shape=jax.ShapeDtypeStruct((8, WIN, col...  2.43 us
  transfers between devices with their start and end apart: 9, of which 4 were waited for; matrix products, arithmetic and copies ran while one was open for 2% of the time, Pallas kernels for 1%

profile of v6, /device:TPU:6, one launch (start us, length us, event | category | flops | bytes accessed | tf_op | source)
XLA Modules:
  0.0 70.9 jit_solution(14482379915264974740)
XLA Ops:
  0.0 0.0 copy-start.1
  0.0 0.0 copy-start
  0.0 2.4 %shard_map.37 = bf16[8,40,256]{2,1,0:T(8,128)(2,1)} custom-call(bf16[384,2048]{1,0:T(8,128)(2,1)} %lower.1, bf16[2048,256]{1,0:T(8,128)(2,1)} %factor.1), custom_call_target="tpu_custom_call" | custom-call | flops 50331648 | bytes 1048576 | tf_op jit(solution)/shard_map/pallas_call | solution.py:66
  2.4 15.6 %all-to-all-start = ((bf16[8,40,256]{2,1,0:T(8,128)(2,1)}), bf16[8,40,256]{2,1,0:T(8,128)(2,1)S(1)}, u32[]{:S(2)}, u32[]{:S(2)}) async-start(bf16[8,40,256]{2,1,0:T(8,128)(2,1)} %shard_map.37), calls=%async_computation | async-start | bytes 327680 | tf_op jit(solution)/shard_map/all_to_all | solution.py:90
  18.1 0.0 copy-done.1
  18.1 0.0 copy-done
  18.1 0.6 convolution_convert_fusion.refs_0_
  18.7 4.9 %collective-permute-start.2 = (bf16[384,256]{1,0:T(8,128)(2,1)S(1)}, bf16[384,256]{1,0:T(8,128)(2,1)S(1)}, u32[]{:S(2)}, u32[]{:S(2)}) collective-permute-start(bf16[384,256]{1,0:T(8,128)(2,1)S(1)} %convolution_convert_fusion.refs_0_), channel_id=1, source_target_pairs={{0,257},{1,256},{256,1},{257,0},{2,259},{3,258},{258,3},{259,2},{4... | collective-permute-start | bytes 589832 | tf_op jit(solution)/shard_map/ppermute | solution.py:96
  23.6 2.5 %collective-permute-start.1 = (bf16[384,256]{1,0:T(8,128)(2,1)S(1)}, bf16[384,256]{1,0:T(8,128)(2,1)S(1)}, u32[]{:S(2)}, u32[]{:S(2)}) collective-permute-start(bf16[384,256]{1,0:T(8,128)(2,1)S(1)} %convolution_convert_fusion.refs_0_), channel_id=1, source_target_pairs={{0,1},{1,0},{2,3},{3,2},{4,5},{5,4},{6,7},{7,6},{8,9},{9,8},{10,11... | collective-permute-start | bytes 589832 | tf_op jit(solution)/shard_map/ppermute | solution.py:95
  26.1 2.4 %collective-permute-start = (bf16[384,256]{1,0:T(8,128)(2,1)S(1)}, bf16[384,256]{1,0:T(8,128)(2,1)S(1)}, u32[]{:S(2)}, u32[]{:S(2)}) collective-permute-start(bf16[384,256]{1,0:T(8,128)(2,1)S(1)} %convolution_convert_fusion.refs_0_), channel_id=1, source_target_pairs={{0,256},{256,0},{1,257},{257,1},{2,258},{258,2},{3,259},{259,3},{4... | collective-permute-start | bytes 589832 | tf_op jit(solution)/shard_map/ppermute | solution.py:94
  28.5 0.2 all-to-all-done
  28.7 0.7 %broadcast_in_dim.2 = bf16[2,2,4,40,256]{4,3,2,1,0:T(8,128)(2,1)} broadcast(bf16[2,4,40,256]{3,2,1,0:T(8,128)(2,1)S(1)} %pad_maximum_fusion.1), dimensions={1,2,3,4} | broadcast | bytes 491520 | tf_op jit(solution)/shard_map/broadcast_in_dim | solution.py:100
  29.5 6.1 %all-to-all-start.1 = ((bf16[4,4,40,256]{3,2,1,0:T(8,128)(2,1)}), bf16[4,4,40,256]{3,2,1,0:T(8,128)(2,1)S(1)}, u32[]{:S(2)}, u32[]{:S(2)}) async-start(bf16[4,4,40,256]{3,2,1,0:T(8,128)(2,1)} %bitcast.5), calls=%async_computation.1 | async-start | bytes 655360 | tf_op jit(solution)/shard_map/all_to_all | solution.py:102
  35.5 0.0 collective-permute-done.2.refs_3_
  35.5 0.0 collective-permute-done.1.refs_2_
  35.5 0.0 collective-permute-done.refs_1_
  35.6 0.1 pad_maximum_fusion
  35.7 1.9 %collective-permute-start.3 = (bf16[4,384,256]{2,1,0:T(8,128)(2,1)S(1)}, bf16[4,384,256]{2,1,0:T(8,128)(2,1)S(1)}, u32[]{:S(2)}, u32[]{:S(2)}) collective-permute-start(bf16[4,384,256]{2,1,0:T(8,128)(2,1)S(1)} %pad_maximum_fusion), channel_id=1, source_target_pairs={{0,128},{128,0},{1,129},{129,1},{2,130},{130,2},{3,131},{131,3},{4... | collective-permute-start | bytes 2359304 | tf_op jit(solution)/shard_map/ppermute | solution.py:98
  37.6 0.1 pad_add_fusion.at_ref
  37.7 0.0 copy-start.2
  37.7 4.9 %all-to-all-done.1.w = bf16[4,4,40,256]{3,2,1,0:T(8,128)(2,1)S(1)} async-done(((bf16[4,4,40,256]{3,2,1,0:T(8,128)(2,1)}), bf16[4,4,40,256]{3,2,1,0:T(8,128)(2,1)S(1)}, u32[]{:S(2)}, u32[]{:S(2)}) %all-to-all-start.1) | async-done | bytes 327712 | tf_op jit(solution)/shard_map/all_to_all | solution.py:102
  42.6 1.0 %shard_map.38 = (f32[80,768]{1,0:T(8,128)S(1)}, f32[80,768]{1,0:T(8,128)S(1)}, f32[80,768]{1,0:T(8,128)S(1)}, f32[80,768]{1,0:T(8,128)S(1)}) custom-call(s32[4]{0:T(128)S(1)} %pad_add_fusion.at_ref, bf16[4,4,40,256]{3,2,1,0:T(8,128)(2,1)S(1)} %all-to-all-done.1.w, bf16[384,256]{1,0:T(8,128)(2,1)S(1)} %convolution_convert_fusion.refs_0_, ...), custom_call_target="tpu_custom_call" | custom-call | flops 251658240 | bytes 2097152 | tf_op jit(solution)/shard_map/pallas_call | solution.py:47
  43.6 0.0 collective-permute-done.3.refs_0_
  43.6 1.1 %shard_map.39 = (f32[80,1536]{1,0:T(8,128)S(1)}, f32[80,1536]{1,0:T(8,128)S(1)}, f32[80,1536]{1,0:T(8,128)S(1)}, f32[80,1536]{1,0:T(8,128)S(1)}) custom-call(s32[4]{0:T(128)S(1)} %pad_add_fusion.at_ref, bf16[4,4,40,256]{3,2,1,0:T(8,128)(2,1)S(1)} %all-to-all-done.1.w, bf16[4,384,256]{2,1,0:T(8,128)(2,1)S(1)} %collective-permute-done.3.refs_0_, ...), custom_call_target="tpu_custom_call" | custom-call | flops 251658240 | bytes 2097152 | tf_op jit(solution)/shard_map/pallas_call | solution.py:47
  44.7 2.4 %collective-permute-start.4 = (f32[80,1536]{1,0:T(8,128)S(1)}, f32[80,1536]{1,0:T(8,128)S(1)}, u32[]{:S(2)}, u32[]{:S(2)}) collective-permute-start(f32[80,1536]{1,0:T(8,128)S(1)} %get-tuple-element.22), channel_id=1, source_target_pairs={{0,2},{2,4},{4,6},{6,0},{1,3},{3,5},{5,7},{7,1},{8,10},{10,12},{12... | collective-permute-start | bytes 1474568 | tf_op jit(solution)/shard_map/ppermute | solution.py:104
  47.1 3.5 %collective-permute-start.5 = (f32[80,1536]{1,0:T(8,128)S(1)}, f32[80,1536]{1,0:T(8,128)S(1)}, u32[]{:S(2)}, u32[]{:S(2)}) collective-permute-start(f32[80,1536]{1,0:T(8,128)S(1)} %get-tuple-element.23), channel_id=1, source_target_pairs={{0,6},{2,0},{4,2},{6,4},{1,7},{3,1},{5,3},{7,5},{8,14},{10,8},{12,... | collective-permute-start | bytes 1474568 | tf_op jit(solution)/shard_map/ppermute | solution.py:104
  50.6 3.3 %collective-permute-start.6 = (f32[80,1536]{1,0:T(8,128)S(1)}, f32[80,1536]{1,0:T(8,128)S(1)}, u32[]{:S(2)}, u32[]{:S(2)}) collective-permute-start(f32[80,1536]{1,0:T(8,128)S(1)} %get-tuple-element.24), channel_id=1, source_target_pairs={{0,4},{2,6},{4,0},{6,2},{1,5},{3,7},{5,1},{7,3},{8,12},{10,14},{12... | collective-permute-start | bytes 1474568 | tf_op jit(solution)/shard_map/ppermute | solution.py:104
  53.9 6.9 %collective-permute-done.4 = f32[80,1536]{1,0:T(8,128)S(1)} collective-permute-done((f32[80,1536]{1,0:T(8,128)S(1)}, f32[80,1536]{1,0:T(8,128)S(1)}, u32[]{:S(2)}, u32[]{:S(2)}) %collective-permute-start.4) | collective-permute-done | bytes 491552 | tf_op jit(solution)/shard_map/ppermute | solution.py:104
  60.8 9.2 %collective-permute-done.5 = f32[80,1536]{1,0:T(8,128)S(1)} collective-permute-done((f32[80,1536]{1,0:T(8,128)S(1)}, f32[80,1536]{1,0:T(8,128)S(1)}, u32[]{:S(2)}, u32[]{:S(2)}) %collective-permute-start.5) | collective-permute-done | bytes 491552 | tf_op jit(solution)/shard_map/ppermute | solution.py:104
  70.0 0.0 collective-permute-done.6
  70.0 0.0 copy-done.2
  70.0 1.0 %add_subtract_fusion = f32[80,1536]{1,0:T(8,128)} fusion(f32[80,1536]{1,0:T(8,128)S(1)} %copy-done.2, f32[80,1536]{1,0:T(8,128)S(1)} %collective-permute-done.5, f32[80,1536]{1,0:T(8,128)S(1)} %collective-permute-done.6, f32[80,1536]{1,0:T(8,128)S(1)} %get-tuple-element.21, f32[80,1536]{1,0:T(8,128)S(1)} %collective-permute-done.4), kind=kLoop, calls=%fused_computation.2 | loop fusion | flops 491520 | bytes 2949120 | tf_op jit(solution)/shard_map/sub | solution.py:105
  (3 shorter events, 0.0 us)
Async XLA Ops:
  0.0 18.1 %copy-start.1 = (bf16[2048,256]{1,0:T(8,128)(2,1)S(1)}, bf16[2048,256]{1,0:T(8,128)(2,1)}, u32[]{:S(2)}) copy-start(bf16[2048,256]{1,0:T(8,128)(2,1)} %factor.1) | copy-start | bytes 3145732
  0.0 18.1 %copy-start = (bf16[384,2048]{1,0:T(8,128)(2,1)S(1)}, bf16[384,2048]{1,0:T(8,128)(2,1)}, u32[]{:S(2)}) copy-start(bf16[384,2048]{1,0:T(8,128)(2,1)} %lower.1) | copy-start | bytes 4718596
  2.4 26.2 %all-to-all-start = ((bf16[8,40,256]{2,1,0:T(8,128)(2,1)}), bf16[8,40,256]{2,1,0:T(8,128)(2,1)S(1)}, u32[]{:S(2)}, u32[]{:S(2)}) async-start(bf16[8,40,256]{2,1,0:T(8,128)(2,1)} %shard_map.37), calls=%async_computation | async-start | bytes 327680 | tf_op jit(solution)/shard_map/all_to_all | solution.py:90
  18.7 16.9 %collective-permute-start.2 = (bf16[384,256]{1,0:T(8,128)(2,1)S(1)}, bf16[384,256]{1,0:T(8,128)(2,1)S(1)}, u32[]{:S(2)}, u32[]{:S(2)}) collective-permute-start(bf16[384,256]{1,0:T(8,128)(2,1)S(1)} %convolution_convert_fusion.refs_0_), channel_id=1, source_target_pairs={{0,257},{1,256},{256,1},{257,0},{2,259},{3,258},{258,3},{259,2},{4... | collective-permute-start | bytes 589832 | tf_op jit(solution)/shard_map/ppermute | solution.py:96
  23.6 11.9 %collective-permute-start.1 = (bf16[384,256]{1,0:T(8,128)(2,1)S(1)}, bf16[384,256]{1,0:T(8,128)(2,1)S(1)}, u32[]{:S(2)}, u32[]{:S(2)}) collective-permute-start(bf16[384,256]{1,0:T(8,128)(2,1)S(1)} %convolution_convert_fusion.refs_0_), channel_id=1, source_target_pairs={{0,1},{1,0},{2,3},{3,2},{4,5},{5,4},{6,7},{7,6},{8,9},{9,8},{10,11... | collective-permute-start | bytes 589832 | tf_op jit(solution)/shard_map/ppermute | solution.py:95
  26.1 9.4 %collective-permute-start = (bf16[384,256]{1,0:T(8,128)(2,1)S(1)}, bf16[384,256]{1,0:T(8,128)(2,1)S(1)}, u32[]{:S(2)}, u32[]{:S(2)}) collective-permute-start(bf16[384,256]{1,0:T(8,128)(2,1)S(1)} %convolution_convert_fusion.refs_0_), channel_id=1, source_target_pairs={{0,256},{256,0},{1,257},{257,1},{2,258},{258,2},{3,259},{259,3},{4... | collective-permute-start | bytes 589832 | tf_op jit(solution)/shard_map/ppermute | solution.py:94
  29.5 13.1 %all-to-all-start.1 = ((bf16[4,4,40,256]{3,2,1,0:T(8,128)(2,1)}), bf16[4,4,40,256]{3,2,1,0:T(8,128)(2,1)S(1)}, u32[]{:S(2)}, u32[]{:S(2)}) async-start(bf16[4,4,40,256]{3,2,1,0:T(8,128)(2,1)} %bitcast.5), calls=%async_computation.1 | async-start | bytes 655360 | tf_op jit(solution)/shard_map/all_to_all | solution.py:102
  35.7 8.0 %collective-permute-start.3 = (bf16[4,384,256]{2,1,0:T(8,128)(2,1)S(1)}, bf16[4,384,256]{2,1,0:T(8,128)(2,1)S(1)}, u32[]{:S(2)}, u32[]{:S(2)}) collective-permute-start(bf16[4,384,256]{2,1,0:T(8,128)(2,1)S(1)} %pad_maximum_fusion), channel_id=1, source_target_pairs={{0,128},{128,0},{1,129},{129,1},{2,130},{130,2},{3,131},{131,3},{4... | collective-permute-start | bytes 2359304 | tf_op jit(solution)/shard_map/ppermute | solution.py:98
  37.7 32.3 %copy-start.2 = (f32[80,1536]{1,0:T(8,128)S(1)}, f32[80,1536]{1,0:T(8,128)}, u32[]{:S(2)}) copy-start(f32[80,1536]{1,0:T(8,128)} %param.5) | copy-start | bytes 1474564
  44.7 16.1 %collective-permute-start.4 = (f32[80,1536]{1,0:T(8,128)S(1)}, f32[80,1536]{1,0:T(8,128)S(1)}, u32[]{:S(2)}, u32[]{:S(2)}) collective-permute-start(f32[80,1536]{1,0:T(8,128)S(1)} %get-tuple-element.22), channel_id=1, source_target_pairs={{0,2},{2,4},{4,6},{6,0},{1,3},{3,5},{5,7},{7,1},{8,10},{10,12},{12... | collective-permute-start | bytes 1474568 | tf_op jit(solution)/shard_map/ppermute | solution.py:104
  47.1 22.8 %collective-permute-start.5 = (f32[80,1536]{1,0:T(8,128)S(1)}, f32[80,1536]{1,0:T(8,128)S(1)}, u32[]{:S(2)}, u32[]{:S(2)}) collective-permute-start(f32[80,1536]{1,0:T(8,128)S(1)} %get-tuple-element.23), channel_id=1, source_target_pairs={{0,6},{2,0},{4,2},{6,4},{1,7},{3,1},{5,3},{7,5},{8,14},{10,8},{12,... | collective-permute-start | bytes 1474568 | tf_op jit(solution)/shard_map/ppermute | solution.py:104
  50.6 19.4 %collective-permute-start.6 = (f32[80,1536]{1,0:T(8,128)S(1)}, f32[80,1536]{1,0:T(8,128)S(1)}, u32[]{:S(2)}, u32[]{:S(2)}) collective-permute-start(f32[80,1536]{1,0:T(8,128)S(1)} %get-tuple-element.24), channel_id=1, source_target_pairs={{0,4},{2,6},{4,0},{6,2},{1,5},{3,7},{5,1},{7,3},{8,12},{10,14},{12... | collective-permute-start | bytes 1474568 | tf_op jit(solution)/shard_map/ppermute | solution.py:104

commit v7 on v6

--- a/solution.py
+++ b/solution.py
@@ -102,7 +102,8 @@
     w = lax.all_to_all(w, ("z", "yhi"), 0, 0, tiled=True, axis_index_groups=fours)
     keep, *send = product(at, w, [theirs], product(at, w, near))
     got = [lax.ppermute(send[k - 1], "x", shift(k)) for k in (2, 1, 3)]
-    return schur_window - ((keep + got[1]) + (got[2] + got[0]))
+    part = lax.optimization_barrier(schur_window - (keep + got[0]))
+    return part - (got[1] + got[2])
 
 
 def solution(mesh):

time: 72.3 us -> 70.2 us (0.971)
  waiting for transfers between devices: 21.1 us -> 19.4 us
    ppermute x3, waiting for transfers between devices: 16 us -> 14.4 us  [on_device(): got = [lax.ppermute(send[k - 1], 'x', shift(k)) for k in (2, 1, 3)]]
  transfers between devices with their start and end apart: 9 -> 9, of which waited for: 4 -> 5; matrix products, arithmetic and copies ran while one was open for 2% -> 2% of each run, Pallas kernels for 1% -> 2%
where the time goes in v7:
time: 70.2 us; the launch traced here: 69.3 us
  starting transfers between devices  42.7 us (61%)
  waiting for transfers between devices  19.4 us (28%)
  Pallas kernels  4.56 us (6%)
  other arithmetic  1.16 us (2%)
  local copies, waits for them, and re-layouts  0.77 us (1%)
    all_to_all x1, starting transfers between devices, on_device(): w = lax.all_to_all(w, 'z', 0, 0, tiled=True, axis_index_groups=groups)  15.6 us
    ppermute x3, waiting for transfers between devices, on_device(): got = [lax.ppermute(send[k - 1], 'x', shift(k)) for k in (2, 1, 3)]  14.4 us
    ppermute x3, starting transfers between devices, on_device(): got = [lax.ppermute(send[k - 1], 'x', shift(k)) for k in (2, 1, 3)]  9.23 us
    all_to_all x1, starting transfers between devices, on_device(): lax.all_to_all(w, ('z', 'yhi'), 0, 0, tiled=True, axis_index_groups=fours)  6.08 us
    ppermute x1, starting transfers between devices, on_device(): lax.ppermute(panel, ('ylo', 'yhi'), [(i, 3 - i) for i in range(4)])  4.92 us
    all_to_all x1, waiting for transfers between devices, on_device(): lax.all_to_all(w, ('z', 'yhi'), 0, 0, tiled=True, axis_index_groups=fours)  4.91 us
    ppermute x1, starting transfers between devices, on_device(): lax.ppermute(panel, 'yhi', SWAP)  2.54 us
    pallas_call x1, Pallas kernels, window(): pl.pallas_call(window_kernel, out_shape=jax.ShapeDtypeStruct((8, WIN, col...  2.43 us
  transfers between devices with their start and end apart: 9, of which 5 were waited for; matrix products, arithmetic and copies ran while one was open for 2% of the time, Pallas kernels for 2%

profile of v7, /device:TPU:6, one launch (start us, length us, event | category | flops | bytes accessed | tf_op | source)
XLA Modules:
  0.0 69.3 jit_solution(7217356791261085323)
XLA Ops:
  0.0 0.0 copy-start.1
  0.0 0.0 copy-start
  0.0 2.4 %shard_map.37 = bf16[8,40,256]{2,1,0:T(8,128)(2,1)} custom-call(bf16[384,2048]{1,0:T(8,128)(2,1)} %lower.1, bf16[2048,256]{1,0:T(8,128)(2,1)} %factor.1), custom_call_target="tpu_custom_call" | custom-call | flops 50331648 | bytes 1048576 | tf_op jit(solution)/shard_map/pallas_call | solution.py:66
  2.4 15.6 %all-to-all-start = ((bf16[8,40,256]{2,1,0:T(8,128)(2,1)}), bf16[8,40,256]{2,1,0:T(8,128)(2,1)S(1)}, u32[]{:S(2)}, u32[]{:S(2)}) async-start(bf16[8,40,256]{2,1,0:T(8,128)(2,1)} %shard_map.37), calls=%async_computation | async-start | bytes 327680 | tf_op jit(solution)/shard_map/all_to_all | solution.py:90
  18.1 0.0 copy-done.1
  18.1 0.0 copy-done
  18.1 0.6 convolution_convert_fusion.refs_0_
  18.7 4.9 %collective-permute-start.2 = (bf16[384,256]{1,0:T(8,128)(2,1)S(1)}, bf16[384,256]{1,0:T(8,128)(2,1)S(1)}, u32[]{:S(2)}, u32[]{:S(2)}) collective-permute-start(bf16[384,256]{1,0:T(8,128)(2,1)S(1)} %convolution_convert_fusion.refs_0_), channel_id=1, source_target_pairs={{0,257},{1,256},{256,1},{257,0},{2,259},{3,258},{258,3},{259,2},{4... | collective-permute-start | bytes 589832 | tf_op jit(solution)/shard_map/ppermute | solution.py:96
  23.6 2.5 %collective-permute-start.1 = (bf16[384,256]{1,0:T(8,128)(2,1)S(1)}, bf16[384,256]{1,0:T(8,128)(2,1)S(1)}, u32[]{:S(2)}, u32[]{:S(2)}) collective-permute-start(bf16[384,256]{1,0:T(8,128)(2,1)S(1)} %convolution_convert_fusion.refs_0_), channel_id=1, source_target_pairs={{0,1},{1,0},{2,3},{3,2},{4,5},{5,4},{6,7},{7,6},{8,9},{9,8},{10,11... | collective-permute-start | bytes 589832 | tf_op jit(solution)/shard_map/ppermute | solution.py:95
  26.1 2.4 %collective-permute-start = (bf16[384,256]{1,0:T(8,128)(2,1)S(1)}, bf16[384,256]{1,0:T(8,128)(2,1)S(1)}, u32[]{:S(2)}, u32[]{:S(2)}) collective-permute-start(bf16[384,256]{1,0:T(8,128)(2,1)S(1)} %convolution_convert_fusion.refs_0_), channel_id=1, source_target_pairs={{0,256},{256,0},{1,257},{257,1},{2,258},{258,2},{3,259},{259,3},{4... | collective-permute-start | bytes 589832 | tf_op jit(solution)/shard_map/ppermute | solution.py:94
  28.5 0.2 all-to-all-done
  28.7 0.7 %broadcast_in_dim.2 = bf16[2,2,4,40,256]{4,3,2,1,0:T(8,128)(2,1)} broadcast(bf16[2,4,40,256]{3,2,1,0:T(8,128)(2,1)S(1)} %pad_maximum_fusion.1), dimensions={1,2,3,4} | broadcast | bytes 491520 | tf_op jit(solution)/shard_map/broadcast_in_dim | solution.py:100
  29.5 6.1 %all-to-all-start.1 = ((bf16[4,4,40,256]{3,2,1,0:T(8,128)(2,1)}), bf16[4,4,40,256]{3,2,1,0:T(8,128)(2,1)S(1)}, u32[]{:S(2)}, u32[]{:S(2)}) async-start(bf16[4,4,40,256]{3,2,1,0:T(8,128)(2,1)} %bitcast.5), calls=%async_computation.1 | async-start | bytes 655360 | tf_op jit(solution)/shard_map/all_to_all | solution.py:102
  35.5 0.0 collective-permute-done.2.refs_3_
  35.5 0.0 collective-permute-done.1.refs_2_
  35.5 0.0 collective-permute-done.refs_1_
  35.6 0.1 pad_maximum_fusion
  35.7 1.9 %collective-permute-start.3 = (bf16[4,384,256]{2,1,0:T(8,128)(2,1)S(1)}, bf16[4,384,256]{2,1,0:T(8,128)(2,1)S(1)}, u32[]{:S(2)}, u32[]{:S(2)}) collective-permute-start(bf16[4,384,256]{2,1,0:T(8,128)(2,1)S(1)} %pad_maximum_fusion), channel_id=1, source_target_pairs={{0,128},{128,0},{1,129},{129,1},{2,130},{130,2},{3,131},{131,3},{4... | collective-permute-start | bytes 2359304 | tf_op jit(solution)/shard_map/ppermute | solution.py:98
  37.6 0.1 pad_add_fusion.at_ref
  37.7 0.0 copy-start.2
  37.7 4.9 %all-to-all-done.1.w = bf16[4,4,40,256]{3,2,1,0:T(8,128)(2,1)S(1)} async-done(((bf16[4,4,40,256]{3,2,1,0:T(8,128)(2,1)}), bf16[4,4,40,256]{3,2,1,0:T(8,128)(2,1)S(1)}, u32[]{:S(2)}, u32[]{:S(2)}) %all-to-all-start.1) | async-done | bytes 327712 | tf_op jit(solution)/shard_map/all_to_all | solution.py:102
  42.6 1.0 %shard_map.38 = (f32[80,768]{1,0:T(8,128)S(1)}, f32[80,768]{1,0:T(8,128)S(1)}, f32[80,768]{1,0:T(8,128)S(1)}, f32[80,768]{1,0:T(8,128)S(1)}) custom-call(s32[4]{0:T(128)S(1)} %pad_add_fusion.at_ref, bf16[4,4,40,256]{3,2,1,0:T(8,128)(2,1)S(1)} %all-to-all-done.1.w, bf16[384,256]{1,0:T(8,128)(2,1)S(1)} %convolution_convert_fusion.refs_0_, ...), custom_call_target="tpu_custom_call" | custom-call | flops 251658240 | bytes 2097152 | tf_op jit(solution)/shard_map/pallas_call | solution.py:47
  43.6 0.0 collective-permute-done.3.refs_0_
  43.6 1.1 %shard_map.39 = (f32[80,1536]{1,0:T(8,128)S(1)}, f32[80,1536]{1,0:T(8,128)S(1)}, f32[80,1536]{1,0:T(8,128)S(1)}, f32[80,1536]{1,0:T(8,128)S(1)}) custom-call(s32[4]{0:T(128)S(1)} %pad_add_fusion.at_ref, bf16[4,4,40,256]{3,2,1,0:T(8,128)(2,1)S(1)} %all-to-all-done.1.w, bf16[4,384,256]{2,1,0:T(8,128)(2,1)S(1)} %collective-permute-done.3.refs_0_, ...), custom_call_target="tpu_custom_call" | custom-call | flops 251658240 | bytes 2097152 | tf_op jit(solution)/shard_map/pallas_call | solution.py:47
  44.7 3.3 %collective-permute-start.4 = (f32[80,1536]{1,0:T(8,128)S(1)}, f32[80,1536]{1,0:T(8,128)S(1)}, u32[]{:S(2)}, u32[]{:S(2)}) collective-permute-start(f32[80,1536]{1,0:T(8,128)S(1)} %get-tuple-element.22), channel_id=1, source_target_pairs={{0,4},{2,6},{4,0},{6,2},{1,5},{3,7},{5,1},{7,3},{8,12},{10,14},{12... | collective-permute-start | bytes 1474568 | tf_op jit(solution)/shard_map/ppermute | solution.py:104
  48.1 4.0 %collective-permute-start.5 = (f32[80,1536]{1,0:T(8,128)S(1)}, f32[80,1536]{1,0:T(8,128)S(1)}, u32[]{:S(2)}, u32[]{:S(2)}) collective-permute-start(f32[80,1536]{1,0:T(8,128)S(1)} %get-tuple-element.23), channel_id=1, source_target_pairs={{0,2},{2,4},{4,6},{6,0},{1,3},{3,5},{5,7},{7,1},{8,10},{10,12},{12... | collective-permute-start | bytes 1474568 | tf_op jit(solution)/shard_map/ppermute | solution.py:104
  52.1 1.9 %collective-permute-start.6 = (f32[80,1536]{1,0:T(8,128)S(1)}, f32[80,1536]{1,0:T(8,128)S(1)}, u32[]{:S(2)}, u32[]{:S(2)}) collective-permute-start(f32[80,1536]{1,0:T(8,128)S(1)} %get-tuple-element.24), channel_id=1, source_target_pairs={{0,6},{2,0},{4,2},{6,4},{1,7},{3,1},{5,3},{7,5},{8,14},{10,8},{12,... | collective-permute-start | bytes 1474568 | tf_op jit(solution)/shard_map/ppermute | solution.py:104
  54.0 8.3 %collective-permute-done.4 = f32[80,1536]{1,0:T(8,128)S(1)} collective-permute-done((f32[80,1536]{1,0:T(8,128)S(1)}, f32[80,1536]{1,0:T(8,128)S(1)}, u32[]{:S(2)}, u32[]{:S(2)}) %collective-permute-start.4) | collective-permute-done | bytes 491552 | tf_op jit(solution)/shard_map/ppermute | solution.py:104
  62.3 0.0 copy-done.2
  62.3 0.1 add_subtract_fusion.1
  62.4 3.5 %collective-permute-done.5 = f32[80,1536]{1,0:T(8,128)S(1)} collective-permute-done((f32[80,1536]{1,0:T(8,128)S(1)}, f32[80,1536]{1,0:T(8,128)S(1)}, u32[]{:S(2)}, u32[]{:S(2)}) %collective-permute-start.5) | collective-permute-done | bytes 491552 | tf_op jit(solution)/shard_map/ppermute | solution.py:104
  65.9 2.5 %collective-permute-done.6 = f32[80,1536]{1,0:T(8,128)S(1)} collective-permute-done((f32[80,1536]{1,0:T(8,128)S(1)}, f32[80,1536]{1,0:T(8,128)S(1)}, u32[]{:S(2)}, u32[]{:S(2)}) %collective-permute-start.6) | collective-permute-done | bytes 491552 | tf_op jit(solution)/shard_map/ppermute | solution.py:104
  68.5 0.9 %add_subtract_fusion = f32[80,1536]{1,0:T(8,128)} fusion(f32[80,1536]{1,0:T(8,128)S(1)} %add_subtract_fusion.1, f32[80,1536]{1,0:T(8,128)S(1)} %collective-permute-done.5, f32[80,1536]{1,0:T(8,128)S(1)} %collective-permute-done.6), kind=kLoop, calls=%fused_computation.2 | loop fusion | flops 245760 | bytes 1966080 | tf_op jit(solution)/shard_map/sub | solution.py:106
  (3 shorter events, 0.0 us)
Async XLA Ops:
  0.0 18.1 %copy-start.1 = (bf16[2048,256]{1,0:T(8,128)(2,1)S(1)}, bf16[2048,256]{1,0:T(8,128)(2,1)}, u32[]{:S(2)}) copy-start(bf16[2048,256]{1,0:T(8,128)(2,1)} %factor.1) | copy-start | bytes 3145732
  0.0 18.1 %copy-start = (bf16[384,2048]{1,0:T(8,128)(2,1)S(1)}, bf16[384,2048]{1,0:T(8,128)(2,1)}, u32[]{:S(2)}) copy-start(bf16[384,2048]{1,0:T(8,128)(2,1)} %lower.1) | copy-start | bytes 4718596
  2.4 26.2 %all-to-all-start = ((bf16[8,40,256]{2,1,0:T(8,128)(2,1)}), bf16[8,40,256]{2,1,0:T(8,128)(2,1)S(1)}, u32[]{:S(2)}, u32[]{:S(2)}) async-start(bf16[8,40,256]{2,1,0:T(8,128)(2,1)} %shard_map.37), calls=%async_computation | async-start | bytes 327680 | tf_op jit(solution)/shard_map/all_to_all | solution.py:90
  18.7 16.9 %collective-permute-start.2 = (bf16[384,256]{1,0:T(8,128)(2,1)S(1)}, bf16[384,256]{1,0:T(8,128)(2,1)S(1)}, u32[]{:S(2)}, u32[]{:S(2)}) collective-permute-start(bf16[384,256]{1,0:T(8,128)(2,1)S(1)} %convolution_convert_fusion.refs_0_), channel_id=1, source_target_pairs={{0,257},{1,256},{256,1},{257,0},{2,259},{3,258},{258,3},{259,2},{4... | collective-permute-start | bytes 589832 | tf_op jit(solution)/shard_map/ppermute | solution.py:96
  23.6 11.9 %collective-permute-start.1 = (bf16[384,256]{1,0:T(8,128)(2,1)S(1)}, bf16[384,256]{1,0:T(8,128)(2,1)S(1)}, u32[]{:S(2)}, u32[]{:S(2)}) collective-permute-start(bf16[384,256]{1,0:T(8,128)(2,1)S(1)} %convolution_convert_fusion.refs_0_), channel_id=1, source_target_pairs={{0,1},{1,0},{2,3},{3,2},{4,5},{5,4},{6,7},{7,6},{8,9},{9,8},{10,11... | collective-permute-start | bytes 589832 | tf_op jit(solution)/shard_map/ppermute | solution.py:95
  26.1 9.4 %collective-permute-start = (bf16[384,256]{1,0:T(8,128)(2,1)S(1)}, bf16[384,256]{1,0:T(8,128)(2,1)S(1)}, u32[]{:S(2)}, u32[]{:S(2)}) collective-permute-start(bf16[384,256]{1,0:T(8,128)(2,1)S(1)} %convolution_convert_fusion.refs_0_), channel_id=1, source_target_pairs={{0,256},{256,0},{1,257},{257,1},{2,258},{258,2},{3,259},{259,3},{4... | collective-permute-start | bytes 589832 | tf_op jit(solution)/shard_map/ppermute | solution.py:94
  29.5 13.1 %all-to-all-start.1 = ((bf16[4,4,40,256]{3,2,1,0:T(8,128)(2,1)}), bf16[4,4,40,256]{3,2,1,0:T(8,128)(2,1)S(1)}, u32[]{:S(2)}, u32[]{:S(2)}) async-start(bf16[4,4,40,256]{3,2,1,0:T(8,128)(2,1)} %bitcast.5), calls=%async_computation.1 | async-start | bytes 655360 | tf_op jit(solution)/shard_map/all_to_all | solution.py:102
  35.7 8.0 %collective-permute-start.3 = (bf16[4,384,256]{2,1,0:T(8,128)(2,1)S(1)}, bf16[4,384,256]{2,1,0:T(8,128)(2,1)S(1)}, u32[]{:S(2)}, u32[]{:S(2)}) collective-permute-start(bf16[4,384,256]{2,1,0:T(8,128)(2,1)S(1)} %pad_maximum_fusion), channel_id=1, source_target_pairs={{0,128},{128,0},{1,129},{129,1},{2,130},{130,2},{3,131},{131,3},{4... | collective-permute-start | bytes 2359304 | tf_op jit(solution)/shard_map/ppermute | solution.py:98
  37.7 24.6 %copy-start.2 = (f32[80,1536]{1,0:T(8,128)S(1)}, f32[80,1536]{1,0:T(8,128)}, u32[]{:S(2)}) copy-start(f32[80,1536]{1,0:T(8,128)} %param.5) | copy-start | bytes 1474564
  44.7 17.6 %collective-permute-start.4 = (f32[80,1536]{1,0:T(8,128)S(1)}, f32[80,1536]{1,0:T(8,128)S(1)}, u32[]{:S(2)}, u32[]{:S(2)}) collective-permute-start(f32[80,1536]{1,0:T(8,128)S(1)} %get-tuple-element.22), channel_id=1, source_target_pairs={{0,4},{2,6},{4,0},{6,2},{1,5},{3,7},{5,1},{7,3},{8,12},{10,14},{12... | collective-permute-start | bytes 1474568 | tf_op jit(solution)/shard_map/ppermute | solution.py:104
  48.1 17.9 %collective-permute-start.5 = (f32[80,1536]{1,0:T(8,128)S(1)}, f32[80,1536]{1,0:T(8,128)S(1)}, u32[]{:S(2)}, u32[]{:S(2)}) collective-permute-start(f32[80,1536]{1,0:T(8,128)S(1)} %get-tuple-element.23), channel_id=1, source_target_pairs={{0,2},{2,4},{4,6},{6,0},{1,3},{3,5},{5,7},{7,1},{8,10},{10,12},{12... | collective-permute-start | bytes 1474568 | tf_op jit(solution)/shard_map/ppermute | solution.py:104
  52.1 16.4 %collective-permute-start.6 = (f32[80,1536]{1,0:T(8,128)S(1)}, f32[80,1536]{1,0:T(8,128)S(1)}, u32[]{:S(2)}, u32[]{:S(2)}) collective-permute-start(f32[80,1536]{1,0:T(8,128)S(1)} %get-tuple-element.24), channel_id=1, source_target_pairs={{0,6},{2,0},{4,2},{6,4},{1,7},{3,1},{5,3},{7,5},{8,14},{10,8},{12,... | collective-permute-start | bytes 1474568 | tf_op jit(solution)/shard_map/ppermute | solution.py:104

commit v8 on v7

--- a/solution.py
+++ b/solution.py
@@ -95,6 +95,7 @@
         lax.ppermute(panel, "yhi", SWAP),
         lax.ppermute(panel, ("ylo", "yhi"), [(i, 3 - i) for i in range(4)]),
     ]
+    near[1], near[2] = lax.optimization_barrier((near[1], near[2]))
     theirs = lax.ppermute(jnp.stack(near), "core", SWAP)
     w = jnp.roll(w.reshape(2, 4, WIN, 256), FIRST // 4, 1)
     w = jnp.broadcast_to(w[None], (2, 2, 4, WIN, 256)).reshape(4, 4, WIN, 256)

time: 70.2 us -> 70.2 us (level)
  no operation moved by 1% of the time
where the time goes in v8:
time: 70.2 us; the launch traced here: 69.3 us
  starting transfers between devices  42.7 us (61%)
  waiting for transfers between devices  19.4 us (28%)
  Pallas kernels  4.56 us (6%)
  other arithmetic  1.16 us (2%)
  local copies, waits for them, and re-layouts  0.77 us (1%)
    all_to_all x1, starting transfers between devices, on_device(): w = lax.all_to_all(w, 'z', 0, 0, tiled=True, axis_index_groups=groups)  15.6 us
    ppermute x3, waiting for transfers between devices, on_device(): got = [lax.ppermute(send[k - 1], 'x', shift(k)) for k in (2, 1, 3)]  14.4 us
    ppermute x3, starting transfers between devices, on_device(): got = [lax.ppermute(send[k - 1], 'x', shift(k)) for k in (2, 1, 3)]  9.23 us
    all_to_all x1, starting transfers between devices, on_device(): lax.all_to_all(w, ('z', 'yhi'), 0, 0, tiled=True, axis_index_groups=fours)  6.08 us
    ppermute x1, starting transfers between devices, on_device(): lax.ppermute(panel, ('ylo', 'yhi'), [(i, 3 - i) for i in range(4)])  4.92 us
    all_to_all x1, waiting for transfers between devices, on_device(): lax.all_to_all(w, ('z', 'yhi'), 0, 0, tiled=True, axis_index_groups=fours)  4.91 us
    ppermute x1, starting transfers between devices, on_device(): lax.ppermute(panel, 'yhi', SWAP)  2.54 us
    pallas_call x1, Pallas kernels, window(): pl.pallas_call(window_kernel, out_shape=jax.ShapeDtypeStruct((8, WIN, col...  2.43 us
  transfers between devices with their start and end apart: 9, of which 5 were waited for; matrix products, arithmetic and copies ran while one was open for 2% of the time, Pallas kernels for 2%

profile of v8, /device:TPU:6, one launch (start us, length us, event | category | flops | bytes accessed | tf_op | source)
XLA Modules:
  0.0 69.3 jit_solution(18435866570017775582)
XLA Ops:
  0.0 0.0 copy-start.1
  0.0 0.0 copy-start
  0.0 2.4 %shard_map.37 = bf16[8,40,256]{2,1,0:T(8,128)(2,1)} custom-call(bf16[384,2048]{1,0:T(8,128)(2,1)} %lower.1, bf16[2048,256]{1,0:T(8,128)(2,1)} %factor.1), custom_call_target="tpu_custom_call" | custom-call | flops 50331648 | bytes 1048576 | tf_op jit(solution)/shard_map/pallas_call | solution.py:66
  2.4 15.6 %all-to-all-start = ((bf16[8,40,256]{2,1,0:T(8,128)(2,1)}), bf16[8,40,256]{2,1,0:T(8,128)(2,1)S(1)}, u32[]{:S(2)}, u32[]{:S(2)}) async-start(bf16[8,40,256]{2,1,0:T(8,128)(2,1)} %shard_map.37), calls=%async_computation | async-start | bytes 327680 | tf_op jit(solution)/shard_map/all_to_all | solution.py:90
  18.1 0.0 copy-done.1
  18.1 0.0 copy-done
  18.1 0.6 convolution_convert_fusion.refs_0_
  18.7 4.9 %collective-permute-start.2 = (bf16[384,256]{1,0:T(8,128)(2,1)S(1)}, bf16[384,256]{1,0:T(8,128)(2,1)S(1)}, u32[]{:S(2)}, u32[]{:S(2)}) collective-permute-start(bf16[384,256]{1,0:T(8,128)(2,1)S(1)} %convolution_convert_fusion.refs_0_), channel_id=1, source_target_pairs={{0,257},{1,256},{256,1},{257,0},{2,259},{3,258},{258,3},{259,2},{4... | collective-permute-start | bytes 589832 | tf_op jit(solution)/shard_map/ppermute | solution.py:96
  23.6 2.5 %collective-permute-start.1 = (bf16[384,256]{1,0:T(8,128)(2,1)S(1)}, bf16[384,256]{1,0:T(8,128)(2,1)S(1)}, u32[]{:S(2)}, u32[]{:S(2)}) collective-permute-start(bf16[384,256]{1,0:T(8,128)(2,1)S(1)} %convolution_convert_fusion.refs_0_), channel_id=1, source_target_pairs={{0,1},{1,0},{2,3},{3,2},{4,5},{5,4},{6,7},{7,6},{8,9},{9,8},{10,11... | collective-permute-start | bytes 589832 | tf_op jit(solution)/shard_map/ppermute | solution.py:95
  26.1 2.4 %collective-permute-start = (bf16[384,256]{1,0:T(8,128)(2,1)S(1)}, bf16[384,256]{1,0:T(8,128)(2,1)S(1)}, u32[]{:S(2)}, u32[]{:S(2)}) collective-permute-start(bf16[384,256]{1,0:T(8,128)(2,1)S(1)} %convolution_convert_fusion.refs_0_), channel_id=1, source_target_pairs={{0,256},{256,0},{1,257},{257,1},{2,258},{258,2},{3,259},{259,3},{4... | collective-permute-start | bytes 589832 | tf_op jit(solution)/shard_map/ppermute | solution.py:94
  28.5 0.2 all-to-all-done
  28.7 0.7 %broadcast_in_dim.2 = bf16[2,2,4,40,256]{4,3,2,1,0:T(8,128)(2,1)} broadcast(bf16[2,4,40,256]{3,2,1,0:T(8,128)(2,1)S(1)} %pad_maximum_fusion.1), dimensions={1,2,3,4} | broadcast | bytes 491520 | tf_op jit(solution)/shard_map/broadcast_in_dim | solution.py:101
  29.5 6.1 %all-to-all-start.1 = ((bf16[4,4,40,256]{3,2,1,0:T(8,128)(2,1)}), bf16[4,4,40,256]{3,2,1,0:T(8,128)(2,1)S(1)}, u32[]{:S(2)}, u32[]{:S(2)}) async-start(bf16[4,4,40,256]{3,2,1,0:T(8,128)(2,1)} %bitcast.5), calls=%async_computation.1 | async-start | bytes 655360 | tf_op jit(solution)/shard_map/all_to_all | solution.py:103
  35.5 0.0 collective-permute-done.1.refs_2_
  35.5 0.0 collective-permute-done.refs_1_
  35.5 0.0 collective-permute-done.2.refs_3_
  35.6 0.1 pad_maximum_fusion
  35.7 1.9 %collective-permute-start.3 = (bf16[4,384,256]{2,1,0:T(8,128)(2,1)S(1)}, bf16[4,384,256]{2,1,0:T(8,128)(2,1)S(1)}, u32[]{:S(2)}, u32[]{:S(2)}) collective-permute-start(bf16[4,384,256]{2,1,0:T(8,128)(2,1)S(1)} %pad_maximum_fusion), channel_id=1, source_target_pairs={{0,128},{128,0},{1,129},{129,1},{2,130},{130,2},{3,131},{131,3},{4... | collective-permute-start | bytes 2359304 | tf_op jit(solution)/shard_map/ppermute | solution.py:99
  37.6 0.1 pad_add_fusion.at_ref
  37.7 0.0 copy-start.2
  37.7 4.9 %all-to-all-done.1.w = bf16[4,4,40,256]{3,2,1,0:T(8,128)(2,1)S(1)} async-done(((bf16[4,4,40,256]{3,2,1,0:T(8,128)(2,1)}), bf16[4,4,40,256]{3,2,1,0:T(8,128)(2,1)S(1)}, u32[]{:S(2)}, u32[]{:S(2)}) %all-to-all-start.1) | async-done | bytes 327712 | tf_op jit(solution)/shard_map/all_to_all | solution.py:103
  42.6 1.0 %shard_map.38 = (f32[80,768]{1,0:T(8,128)S(1)}, f32[80,768]{1,0:T(8,128)S(1)}, f32[80,768]{1,0:T(8,128)S(1)}, f32[80,768]{1,0:T(8,128)S(1)}) custom-call(s32[4]{0:T(128)S(1)} %pad_add_fusion.at_ref, bf16[4,4,40,256]{3,2,1,0:T(8,128)(2,1)S(1)} %all-to-all-done.1.w, bf16[384,256]{1,0:T(8,128)(2,1)S(1)} %convolution_convert_fusion.refs_0_, ...), custom_call_target="tpu_custom_call" | custom-call | flops 251658240 | bytes 2097152 | tf_op jit(solution)/shard_map/pallas_call | solution.py:47
  43.6 0.0 collective-permute-done.3.refs_0_
  43.6 1.1 %shard_map.39 = (f32[80,1536]{1,0:T(8,128)S(1)}, f32[80,1536]{1,0:T(8,128)S(1)}, f32[80,1536]{1,0:T(8,128)S(1)}, f32[80,1536]{1,0:T(8,128)S(1)}) custom-call(s32[4]{0:T(128)S(1)} %pad_add_fusion.at_ref, bf16[4,4,40,256]{3,2,1,0:T(8,128)(2,1)S(1)} %all-to-all-done.1.w, bf16[4,384,256]{2,1,0:T(8,128)(2,1)S(1)} %collective-permute-done.3.refs_0_, ...), custom_call_target="tpu_custom_call" | custom-call | flops 251658240 | bytes 2097152 | tf_op jit(solution)/shard_map/pallas_call | solution.py:47
  44.7 3.3 %collective-permute-start.4 = (f32[80,1536]{1,0:T(8,128)S(1)}, f32[80,1536]{1,0:T(8,128)S(1)}, u32[]{:S(2)}, u32[]{:S(2)}) collective-permute-start(f32[80,1536]{1,0:T(8,128)S(1)} %get-tuple-element.26), channel_id=1, source_target_pairs={{0,4},{2,6},{4,0},{6,2},{1,5},{3,7},{5,1},{7,3},{8,12},{10,14},{12... | collective-permute-start | bytes 1474568 | tf_op jit(solution)/shard_map/ppermute | solution.py:105
  48.1 4.0 %collective-permute-start.5 = (f32[80,1536]{1,0:T(8,128)S(1)}, f32[80,1536]{1,0:T(8,128)S(1)}, u32[]{:S(2)}, u32[]{:S(2)}) collective-permute-start(f32[80,1536]{1,0:T(8,128)S(1)} %get-tuple-element.27), channel_id=1, source_target_pairs={{0,2},{2,4},{4,6},{6,0},{1,3},{3,5},{5,7},{7,1},{8,10},{10,12},{12... | collective-permute-start | bytes 1474568 | tf_op jit(solution)/shard_map/ppermute | solution.py:105
  52.1 1.9 %collective-permute-start.6 = (f32[80,1536]{1,0:T(8,128)S(1)}, f32[80,1536]{1,0:T(8,128)S(1)}, u32[]{:S(2)}, u32[]{:S(2)}) collective-permute-start(f32[80,1536]{1,0:T(8,128)S(1)} %get-tuple-element.28), channel_id=1, source_target_pairs={{0,6},{2,0},{4,2},{6,4},{1,7},{3,1},{5,3},{7,5},{8,14},{10,8},{12,... | collective-permute-start | bytes 1474568 | tf_op jit(solution)/shard_map/ppermute | solution.py:105
  54.0 8.3 %collective-permute-done.4 = f32[80,1536]{1,0:T(8,128)S(1)} collective-permute-done((f32[80,1536]{1,0:T(8,128)S(1)}, f32[80,1536]{1,0:T(8,128)S(1)}, u32[]{:S(2)}, u32[]{:S(2)}) %collective-permute-start.4) | collective-permute-done | bytes 491552 | tf_op jit(solution)/shard_map/ppermute | solution.py:105
  62.3 0.0 copy-done.2
  62.3 0.1 add_subtract_fusion.1
  62.4 3.5 %collective-permute-done.5 = f32[80,1536]{1,0:T(8,128)S(1)} collective-permute-done((f32[80,1536]{1,0:T(8,128)S(1)}, f32[80,1536]{1,0:T(8,128)S(1)}, u32[]{:S(2)}, u32[]{:S(2)}) %collective-permute-start.5) | collective-permute-done | bytes 491552 | tf_op jit(solution)/shard_map/ppermute | solution.py:105
  65.9 2.5 %collective-permute-done.6 = f32[80,1536]{1,0:T(8,128)S(1)} collective-permute-done((f32[80,1536]{1,0:T(8,128)S(1)}, f32[80,1536]{1,0:T(8,128)S(1)}, u32[]{:S(2)}, u32[]{:S(2)}) %collective-permute-start.6) | collective-permute-done | bytes 491552 | tf_op jit(solution)/shard_map/ppermute | solution.py:105
  68.5 0.9 %add_subtract_fusion = f32[80,1536]{1,0:T(8,128)} fusion(f32[80,1536]{1,0:T(8,128)S(1)} %add_subtract_fusion.1, f32[80,1536]{1,0:T(8,128)S(1)} %collective-permute-done.5, f32[80,1536]{1,0:T(8,128)S(1)} %collective-permute-done.6), kind=kLoop, calls=%fused_computation.2 | loop fusion | flops 245760 | bytes 1966080 | tf_op jit(solution)/shard_map/sub | solution.py:107
  (3 shorter events, 0.0 us)
Async XLA Ops:
  0.0 18.1 %copy-start.1 = (bf16[2048,256]{1,0:T(8,128)(2,1)S(1)}, bf16[2048,256]{1,0:T(8,128)(2,1)}, u32[]{:S(2)}) copy-start(bf16[2048,256]{1,0:T(8,128)(2,1)} %factor.1) | copy-start | bytes 3145732
  0.0 18.1 %copy-start = (bf16[384,2048]{1,0:T(8,128)(2,1)S(1)}, bf16[384,2048]{1,0:T(8,128)(2,1)}, u32[]{:S(2)}) copy-start(bf16[384,2048]{1,0:T(8,128)(2,1)} %lower.1) | copy-start | bytes 4718596
  2.4 26.2 %all-to-all-start = ((bf16[8,40,256]{2,1,0:T(8,128)(2,1)}), bf16[8,40,256]{2,1,0:T(8,128)(2,1)S(1)}, u32[]{:S(2)}, u32[]{:S(2)}) async-start(bf16[8,40,256]{2,1,0:T(8,128)(2,1)} %shard_map.37), calls=%async_computation | async-start | bytes 327680 | tf_op jit(solution)/shard_map/all_to_all | solution.py:90
  18.7 16.9 %collective-permute-start.2 = (bf16[384,256]{1,0:T(8,128)(2,1)S(1)}, bf16[384,256]{1,0:T(8,128)(2,1)S(1)}, u32[]{:S(2)}, u32[]{:S(2)}) collective-permute-start(bf16[384,256]{1,0:T(8,128)(2,1)S(1)} %convolution_convert_fusion.refs_0_), channel_id=1, source_target_pairs={{0,257},{1,256},{256,1},{257,0},{2,259},{3,258},{258,3},{259,2},{4... | collective-permute-start | bytes 589832 | tf_op jit(solution)/shard_map/ppermute | solution.py:96
  23.6 11.9 %collective-permute-start.1 = (bf16[384,256]{1,0:T(8,128)(2,1)S(1)}, bf16[384,256]{1,0:T(8,128)(2,1)S(1)}, u32[]{:S(2)}, u32[]{:S(2)}) collective-permute-start(bf16[384,256]{1,0:T(8,128)(2,1)S(1)} %convolution_convert_fusion.refs_0_), channel_id=1, source_target_pairs={{0,1},{1,0},{2,3},{3,2},{4,5},{5,4},{6,7},{7,6},{8,9},{9,8},{10,11... | collective-permute-start | bytes 589832 | tf_op jit(solution)/shard_map/ppermute | solution.py:95
  26.1 9.4 %collective-permute-start = (bf16[384,256]{1,0:T(8,128)(2,1)S(1)}, bf16[384,256]{1,0:T(8,128)(2,1)S(1)}, u32[]{:S(2)}, u32[]{:S(2)}) collective-permute-start(bf16[384,256]{1,0:T(8,128)(2,1)S(1)} %convolution_convert_fusion.refs_0_), channel_id=1, source_target_pairs={{0,256},{256,0},{1,257},{257,1},{2,258},{258,2},{3,259},{259,3},{4... | collective-permute-start | bytes 589832 | tf_op jit(solution)/shard_map/ppermute | solution.py:94
  29.5 13.1 %all-to-all-start.1 = ((bf16[4,4,40,256]{3,2,1,0:T(8,128)(2,1)}), bf16[4,4,40,256]{3,2,1,0:T(8,128)(2,1)S(1)}, u32[]{:S(2)}, u32[]{:S(2)}) async-start(bf16[4,4,40,256]{3,2,1,0:T(8,128)(2,1)} %bitcast.5), calls=%async_computation.1 | async-start | bytes 655360 | tf_op jit(solution)/shard_map/all_to_all | solution.py:103
  35.7 8.0 %collective-permute-start.3 = (bf16[4,384,256]{2,1,0:T(8,128)(2,1)S(1)}, bf16[4,384,256]{2,1,0:T(8,128)(2,1)S(1)}, u32[]{:S(2)}, u32[]{:S(2)}) collective-permute-start(bf16[4,384,256]{2,1,0:T(8,128)(2,1)S(1)} %pad_maximum_fusion), channel_id=1, source_target_pairs={{0,128},{128,0},{1,129},{129,1},{2,130},{130,2},{3,131},{131,3},{4... | collective-permute-start | bytes 2359304 | tf_op jit(solution)/shard_map/ppermute | solution.py:99
  37.7 24.6 %copy-start.2 = (f32[80,1536]{1,0:T(8,128)S(1)}, f32[80,1536]{1,0:T(8,128)}, u32[]{:S(2)}) copy-start(f32[80,1536]{1,0:T(8,128)} %param.5) | copy-start | bytes 1474564
  44.7 17.6 %collective-permute-start.4 = (f32[80,1536]{1,0:T(8,128)S(1)}, f32[80,1536]{1,0:T(8,128)S(1)}, u32[]{:S(2)}, u32[]{:S(2)}) collective-permute-start(f32[80,1536]{1,0:T(8,128)S(1)} %get-tuple-element.26), channel_id=1, source_target_pairs={{0,4},{2,6},{4,0},{6,2},{1,5},{3,7},{5,1},{7,3},{8,12},{10,14},{12... | collective-permute-start | bytes 1474568 | tf_op jit(solution)/shard_map/ppermute | solution.py:105
  48.1 17.9 %collective-permute-start.5 = (f32[80,1536]{1,0:T(8,128)S(1)}, f32[80,1536]{1,0:T(8,128)S(1)}, u32[]{:S(2)}, u32[]{:S(2)}) collective-permute-start(f32[80,1536]{1,0:T(8,128)S(1)} %get-tuple-element.27), channel_id=1, source_target_pairs={{0,2},{2,4},{4,6},{6,0},{1,3},{3,5},{5,7},{7,1},{8,10},{10,12},{12... | collective-permute-start | bytes 1474568 | tf_op jit(solution)/shard_map/ppermute | solution.py:105
  52.1 16.4 %collective-permute-start.6 = (f32[80,1536]{1,0:T(8,128)S(1)}, f32[80,1536]{1,0:T(8,128)S(1)}, u32[]{:S(2)}, u32[]{:S(2)}) collective-permute-start(f32[80,1536]{1,0:T(8,128)S(1)} %get-tuple-element.28), channel_id=1, source_target_pairs={{0,6},{2,0},{4,2},{6,4},{1,7},{3,1},{5,3},{7,5},{8,14},{10,8},{12,... | collective-permute-start | bytes 1474568 | tf_op jit(solution)/shard_map/ppermute | solution.py:105
